TPU v7x, 512 devices: a whole 4x4x16 slice. The times are simulated.
512 devices in a mesh: rows: 32 (over y, x, core), heads: 16 (over z).
Axes of the slice: x: 4, y: 4, z: 16, core: 2. Of those that a mesh axis runs over, the one named last changes fastest.
Arguments:
- pixels: float32 [8192, 768], P('rows'), may hold values from -6 to 6
- perturbation: float32 [8192, 768], P('rows'), may hold values from -0.6 to 0.6
- segment_ids: int32 [32, 256], P('rows'), may hold values from 0 to 3, never falling along the last dimension, each value on 1 to 128 neighbouring positions
- ball_radius: float32 [32, 4], P('rows'), may hold values from 0.05 to 0.4
- w_embed: bfloat16 [768, 1024], replicated, may hold values from -0.21875 to 0.21875
- gain_attn: float32 [1024], replicated, may hold values from 0.5 to 1.5
- w_qkv: bfloat16 [1024, 3, 1024], P('rows', None, 'heads'), may hold values from -0.1875 to 0.1875
- w_out: bfloat16 [1024, 1024], P('heads', 'rows'), may hold values from -0.1875 to 0.1875
- gain_mlp: float32 [1024], replicated, may hold values from 0.5 to 1.5
- w_up: bfloat16 [1024, 4096], P('rows', 'heads'), may hold values from -0.1875 to 0.1875
- w_down: bfloat16 [4096, 1024], P('heads', 'rows'), may hold values from -0.09375 to 0.09375
- out_grad: bfloat16 [8192, 1024], P('rows'), may hold values from -6 to 6
Outputs:
- block_out: bfloat16 [8192, 1024], P('rows')
- new_perturbation: float32 [8192, 768], P('rows')
Inputs may be any that keep to these rules, and one draw needn't show every extreme that they name: `segment_ids`: each pack numbers its images 0 to 3 in order along the pack; each image has 1 to 128 patches and some image of every pack has exactly 128.
All inputs are finite; a program needn't handle non-finite values.
Results may differ from a plain program's by a relative error of at most 0.019.
Values may be sent and summed in bfloat16 or wider, within the bound.
No kernel may reach another device: no remote copies, remote signals or barrier semaphores. Data moves between devices by JAX's collectives and lax.ppermute only.
A program may use at most 64 MiB of HBM per device.

v0:
```python
import math

import jax
import jax.numpy as jnp
from jax import lax
from jax.sharding import PartitionSpec as P

D = 1024
HEADS = 16


STEP_SIZE = 0.1


def layer_norm(values, gain):
    center = jnp.mean(values, -1, keepdims=True)
    shifted = values - center
    spread = jnp.mean(shifted * shifted, -1, keepdims=True)
    return shifted * lax.rsqrt(spread + 1e-05) * gain


def norm_back(values, gain, upstream):
    _, pull = jax.vjp(lambda t: layer_norm(t, gain), values)
    return pull(upstream)[0]


def gelu_back(values, upstream):
    _, pull = jax.vjp(jax.nn.gelu, values)
    return pull(upstream)[0]


def split_heads(projected):
    count, _, width = projected.shape
    size = D // HEADS
    parts = projected.reshape(count, 3, width // size, size)
    return (parts[:, 0], parts[:, 1], parts[:, 2])


def attend(projected, same):
    count, _, width = projected.shape
    query, keys, values = split_heads(projected)
    scale = 1.0 / math.sqrt(D // HEADS)
    scores = jnp.einsum("qhd,khd->hqk", query, keys, preferred_element_type=jnp.float32) * scale
    powers = jnp.where(same[None], jnp.exp(scores), 0.0)
    shares = powers / jnp.sum(powers, -1, keepdims=True)
    shares_low = shares.astype(jnp.bfloat16)
    mixed = jnp.einsum("hqk,khd->qhd", shares_low, values, preferred_element_type=jnp.float32)
    return (mixed.astype(jnp.bfloat16).reshape(count, width), shares, shares_low)


def attend_back(grad_heads, projected, shares, shares_low):
    count, _, width = projected.shape
    query, keys, values = split_heads(projected)
    size = D // HEADS
    scale = 1.0 / math.sqrt(size)
    upstream = grad_heads.reshape(count, width // size, size)
    grad_shares = jnp.einsum("qhd,khd->hqk", upstream, values, preferred_element_type=jnp.float32)
    grad_value = jnp.einsum(
        "hqk,qhd->khd", shares_low, upstream, preferred_element_type=jnp.float32
    ).astype(jnp.bfloat16)
    inner = jnp.sum(grad_shares * shares, -1, keepdims=True)
    grad_scores = (shares * (grad_shares - inner) * scale).astype(jnp.bfloat16)
    grad_query = jnp.einsum(
        "hqk,khd->qhd", grad_scores, keys, preferred_element_type=jnp.float32
    ).astype(jnp.bfloat16)
    grad_key = jnp.einsum(
        "hqk,qhd->khd", grad_scores, query, preferred_element_type=jnp.float32
    ).astype(jnp.bfloat16)
    return jnp.stack([grad_query, grad_key, grad_value], 1).reshape(count, 3, width)


def body(
    pixels,
    perturbation,
    segment_ids,
    ball_radius,
    w_embed,
    gain_attn,
    w_qkv,
    w_out,
    gain_mlp,
    w_up,
    w_down,
    out_grad,
):
    local_rows = pixels.shape[0]
    images = ball_radius.shape[1]
    patch_size = pixels.shape[1]
    w_qkv, w_out, w_up, w_down = (
        lax.all_gather(w_qkv, "rows", axis=0, tiled=True),
        lax.all_gather(w_out, "rows", axis=1, tiled=True),
        lax.all_gather(w_up, "rows", axis=0, tiled=True),
        lax.all_gather(w_down, "rows", axis=1, tiled=True),
    )
    model = w_qkv.shape[0]
    share = w_qkv.shape[2]
    labels = segment_ids[0]
    same = labels[:, None] == labels[None, :]
    inputs = (pixels + perturbation).astype(jnp.bfloat16)
    embedded = jnp.dot(inputs, w_embed, preferred_element_type=jnp.float32)
    normed_one = layer_norm(embedded, gain_attn).astype(jnp.bfloat16)
    projected = jnp.dot(
        normed_one, w_qkv.reshape(model, 3 * share), preferred_element_type=jnp.float32
    )
    projected = projected.reshape(local_rows, 3, share).astype(jnp.bfloat16)
    attended, shares, shares_low = attend(projected, same)
    attn_terms = jnp.dot(attended, w_out, preferred_element_type=jnp.float32)
    stream_mid = embedded + lax.psum(attn_terms.astype(jnp.bfloat16), "heads").astype(jnp.float32)
    normed_two = layer_norm(stream_mid, gain_mlp).astype(jnp.bfloat16)
    hidden_pre = jnp.dot(normed_two, w_up, preferred_element_type=jnp.float32)
    hidden_act = jax.nn.gelu(hidden_pre).astype(jnp.bfloat16)
    mlp_terms = jnp.dot(hidden_act, w_down, preferred_element_type=jnp.float32)
    stream_out = stream_mid + lax.psum(mlp_terms.astype(jnp.bfloat16), "heads").astype(jnp.float32)
    grad_hidden = jnp.dot(out_grad, w_down.T, preferred_element_type=jnp.float32)
    grad_pre = gelu_back(hidden_pre, grad_hidden).astype(jnp.bfloat16)
    up_terms = jnp.dot(grad_pre, w_up.T, preferred_element_type=jnp.float32)
    grad_norm_two = lax.psum(up_terms.astype(jnp.bfloat16), "heads").astype(jnp.float32)
    grad_mid = out_grad.astype(jnp.float32) + norm_back(stream_mid, gain_mlp, grad_norm_two)
    grad_mid_low = grad_mid.astype(jnp.bfloat16)
    grad_heads = jnp.dot(grad_mid_low, w_out.T, preferred_element_type=jnp.float32).astype(
        jnp.bfloat16
    )
    grad_proj = attend_back(grad_heads, projected, shares, shares_low)
    qkv_terms = jnp.einsum("tcf,dcf->td", grad_proj, w_qkv, preferred_element_type=jnp.float32)
    grad_norm_one = lax.psum(qkv_terms.astype(jnp.bfloat16), "heads").astype(jnp.float32)
    grad_embed = grad_mid + norm_back(embedded, gain_attn, grad_norm_one)
    grad_input = jnp.dot(
        grad_embed.astype(jnp.bfloat16), w_embed.T, preferred_element_type=jnp.float32
    )
    numbers = jnp.arange(images, dtype=jnp.int32)
    onehot = (labels[:, None] == numbers[None, :]).astype(jnp.float32)
    counts = jnp.sum(onehot, 0) * patch_size
    grad_sq = jnp.sum(onehot * jnp.sum(grad_input * grad_input, 1)[:, None], 0)
    scale = STEP_SIZE * lax.rsqrt(grad_sq / counts + 1e-06)
    candidate = perturbation + jnp.sum(onehot * scale[None, :], 1)[:, None] * grad_input
    cand_sq = jnp.sum(onehot * jnp.sum(candidate * candidate, 1)[:, None], 0)
    factor = jnp.minimum(1.0, ball_radius[0] * lax.rsqrt(cand_sq / counts + 1e-06))
    updated = candidate * jnp.sum(onehot * factor[None, :], 1)[:, None]
    return (stream_out.astype(jnp.bfloat16), updated)


def solution(mesh):
    in_specs = (
        P("rows", None),
        P("rows", None),
        P("rows", None),
        P("rows", None),
        P(),
        P(),
        P("rows", None, "heads"),
        P("heads", "rows"),
        P(),
        P("rows", "heads"),
        P("heads", "rows"),
        P("rows", None),
    )
    out_specs = (P("rows", None), P("rows", None))
    return jax.shard_map(body, mesh=mesh, in_specs=in_specs, out_specs=out_specs, check_vma=False)
```

profile of v0, /device:TPU:1, one launch (start us, length us, event | category | flops | bytes accessed | tf_op | source)
XLA Modules:
  0.0 492.1 jit_solution(2549400492572858672)
XLA Ops:
  7.2 32.0 %all_gather.13 = bf16[64,1024]{0,1:T(8,128)(2,1)} all-gather(bf16[64,32]{0,1:T(8,128)(2,1)} %param.19), channel_id=1, replica_groups=mesh['rows'=32,'heads'=16] {'rows'}, dimensions={1}, use_global_device_ids=true | all-gather | bytes 135168 | tf_op jit(solution)/shard_map/all_gather | solution.py:91
  39.2 23.7 %all_gather.12 = bf16[1024,3,64]{2,0,1:T(8,128)(2,1)S(1)} all-gather(bf16[32,3,64]{2,0,1:T(8,128)(2,1)} %param.18), channel_id=1, replica_groups=mesh['rows'=32,'heads'=16] {'rows'}, dimensions={0}, use_global_device_ids=true | all-gather | bytes 405504 | tf_op jit(solution)/shard_map/all_gather | solution.py:90
  62.9 0.9 copy-done.4
  63.8 1.0 copy.15
  64.9 1.8 fusion.69
  67.4 1.6 fusion.70
  69.0 2.3 convolution_convert_fusion.2
  71.4 25.3 %all_gather.14 = bf16[1024,256]{1,0:T(8,128)(2,1)} all-gather(bf16[32,256]{1,0:T(8,128)(2,1)S(1)} %copy-done.18), channel_id=1, replica_groups=mesh['rows'=32,'heads'=16] {'rows'}, dimensions={0}, use_global_device_ids=true | all-gather | bytes 540672 | tf_op jit(solution)/shard_map/all_gather | solution.py:92
  96.7 25.8 %all_gather.15 = bf16[256,1024]{0,1:T(8,128)(2,1)} all-gather(bf16[256,32]{0,1:T(8,128)(2,1)S(1)} %copy-done.19), channel_id=1, replica_groups=mesh['rows'=32,'heads'=16] {'rows'}, dimensions={1}, use_global_device_ids=true | all-gather | bytes 540672 | tf_op jit(solution)/shard_map/all_gather | solution.py:93
  122.6 74.5 %all-reduce.5.cloned.1.call-done = bf16[256,1024]{1,0:T(8,128)(2,1)} async-done(((bf16[256,1024]{1,0:T(8,128)(2,1)}), bf16[256,1024]{1,0:T(8,128)(2,1)}) %all-reduce.5.cloned.1.call-update) | async-done | bytes 524304 | tf_op jit(solution)/shard_map/psum | solution.py:108
  197.0 1.3 fusion.68
  198.6 0.7 copy-done.1
  199.3 1.1 fusion.12
  200.4 3.0 convolution_convert_fusion
  203.6 2.3 convolution_convert_fusion.1
  205.9 131.2 %all-reduce.7.cloned.1.call-done = bf16[256,1024]{1,0:T(8,128)(2,1)} async-done(((bf16[256,1024]{1,0:T(8,128)(2,1)}), bf16[256,1024]{1,0:T(8,128)(2,1)}) %all-reduce.7.cloned.1.call-update) | async-done | bytes 524304 | tf_op jit(solution)/shard_map/psum | solution.py:117
  337.1 1.8 multiply_reduce_fusion.1
  339.4 0.5 copy-done.12
  341.7 1.3 fusion
  343.0 135.7 %all-reduce.9.cloned.1.call-done = (bf16[256,1024]{1,0:T(8,128)(2,1)}, bf16[256,1024]{1,0:T(8,128)(2,1)}) async-done(((bf16[256,1024]{1,0:T(8,128)(2,1)}, bf16[256,1024]{1,0:T(8,128)(2,1)}), (bf16[256,1024]{1,0:T(8,128)(2,1)}, bf16[256,1024]{1,0:T(8,128)(2,1)})) %all-reduce.9.cloned.1.call-update) | async-done | bytes 1048592 | tf_op jit(solution)/shard_map/psum | solution.py:113
  478.6 2.7 multiply_reduce_fusion
  481.8 0.7 copy-done.7
  482.7 1.0 multiply_reduce_fusion.5
  484.5 1.1 broadcast_multiply_fusion
  (84 shorter events, 4.9 us)
Async XLA Ops:
  7.2 57.7 %copy-start = (bf16[768,1024]{1,0:T(8,128)(2,1)S(1)}, bf16[768,1024]{1,0:T(8,128)(2,1)}, u32[]{:S(2)}) copy-start(bf16[768,1024]{1,0:T(8,128)(2,1)} %param.16) | copy-start | bytes 4718596
  7.2 57.7 %copy-start.3 = (f32[256,768]{1,0:T(8,128)S(1)}, f32[256,768]{1,0:T(8,128)}, u32[]{:S(2)}) copy-start(f32[256,768]{1,0:T(8,128)} %param.13) | copy-start | bytes 2359300
  7.2 189.8 %all-reduce.5.cloned.1.call-start = ((), (), s32[]{:S(2)}) async-start(), calls=%async_computation | async-start | bytes 1048576 | tf_op jit(solution)/shard_map/psum | solution.py:108
  64.8 2.1 copy-start.11
  64.8 2.2 copy-start.17
  67.0 2.0 copy-start.24
  67.0 4.3 copy-start.22
  67.0 4.4 copy-start.18
  67.4 29.3 %copy-start.19 = (bf16[256,32]{0,1:T(8,128)(2,1)S(1)}, bf16[256,32]{0,1:T(8,128)(2,1)}, u32[]{:S(2)}) copy-start(bf16[256,32]{0,1:T(8,128)(2,1)} %param.22) | copy-start | bytes 49156
  71.3 265.7 %all-reduce.7.cloned.1.call-start = ((), (), s32[]{:S(2)}) async-start(), calls=%async_computation.1 | async-start | bytes 1048576 | tf_op jit(solution)/shard_map/psum | solution.py:117
  122.6 76.7 %copy-start.16 = (f32[1024]{0:T(1024)S(1)}, f32[1024]{0:T(1024)}, u32[]{:S(2)}) copy-start(f32[1024]{0:T(1024)} %param.20) | copy-start | bytes 12292
  197.0 2.3 copy-start.10
  203.4 275.2 %all-reduce.9.cloned.1.call-start = ((), (), s32[]{:S(2)}) async-start(), calls=%async_computation.2 | async-start | bytes 2097152 | tf_op jit(solution)/shard_map/psum | solution.py:113
  337.1 1.8 copy-start.2
  337.1 1.8 copy-start.8
  339.3 1.6 copy-start.6
  339.4 1.2 copy-start.15
  339.4 1.2 copy-start.26
  340.5 1.1 copy-start.5
  478.6 2.7 copy-start.25
  478.6 2.7 copy-start.9
  478.6 2.8 copy-start.23
  481.4 1.2 copy-start.7
  481.4 1.4 copy-start.14
  (7 other events, 6.4 us)
Sparse Core Ops, SparseCore 0:
  71.5 125.5 all-reduce.4
  203.5 133.5 all-reduce.6
  343.1 135.5 all-reduce.8
where the time goes:
time: 502 us; the launch traced here: 492 us
  waiting for transfers between devices  341 us (68%)
  blocking collectives  107 us (21%)
  matrix products  15.9 us (3%)
  between operations  14.1 us (3%)
  other arithmetic  9.03 us (2%)
    psum x1, waiting for transfers between devices, body(): lax.psum(mlp_terms.astype(jnp.bfloat16), 'heads').astype(jnp.float32)  136 us
    psum x1, waiting for transfers between devices, body(): lax.psum(up_terms.astype(jnp.bfloat16), 'heads').astype(jnp.float32)  131 us
    psum x1, waiting for transfers between devices, body(): lax.psum(attn_terms.astype(jnp.bfloat16), 'heads').astype(jnp.float32)  74.5 us
    all_gather x1, blocking collectives, body(): lax.all_gather(w_out, 'rows', axis=1, tiled=True)  32 us
    all_gather x1, blocking collectives, body(): lax.all_gather(w_down, 'rows', axis=1, tiled=True)  25.8 us
    all_gather x1, blocking collectives, body(): lax.all_gather(w_up, 'rows', axis=0, tiled=True)  25.3 us
    all_gather x1, blocking collectives, body(): lax.all_gather(w_qkv, 'rows', axis=0, tiled=True)  23.7 us
  transfers between devices with their start and end apart: 3, of which 3 were waited for; matrix products, arithmetic and copies ran while one was open for 0% of the time, Pallas kernels for 0%

commit v1 on v0

v1 whole, which is shorter than its diff:
```python
import math

import jax
import jax.numpy as jnp
from jax import lax
from jax.experimental import pallas as pl
from jax.experimental.pallas import tpu as pltpu
from jax.sharding import PartitionSpec as P

HEADS = 16
STEP_SIZE = 0.1
VMEM_LIMIT = 56 * 1024 * 1024
F32 = jnp.float32
BF16 = jnp.bfloat16


def mm(a, b):
    return lax.dot_general(a, b, (((1,), (0,)), ((), ())), preferred_element_type=F32)


def mm_nt(a, b):
    return lax.dot_general(a, b, (((1,), (1,)), ((), ())), preferred_element_type=F32)


def mm_tn(a, b):
    return lax.dot_general(a, b, (((0,), (0,)), ((), ())), preferred_element_type=F32)


def normalize(values):
    center = jnp.mean(values, -1, keepdims=True)
    shifted = values - center
    spread = jnp.mean(shifted * shifted, -1, keepdims=True)
    inv = lax.rsqrt(spread + 1e-05)
    return shifted * inv, inv


def norm_back(values, gain, upstream):
    hat, inv = normalize(values)
    scaled = upstream * gain
    return inv * (
        scaled
        - jnp.mean(scaled, -1, keepdims=True)
        - hat * jnp.mean(scaled * hat, -1, keepdims=True)
    )


def head_mask(shape, head, size):
    lane = lax.broadcasted_iota(jnp.int32, shape, 1)
    return (lane >= head * size) & (lane < (head + 1) * size)


def softmax_shares(query, keys, same, scale):
    scores = mm_nt(query, keys) * scale
    powers = jnp.where(same, jnp.exp(scores), 0.0)
    return powers * (1.0 / jnp.sum(powers, -1, keepdims=True))


def attention_kernel(
    size,
    pix_ref, pert_ref, emb_w_ref, gain1_ref, gain2_ref, col_ref, row_ref,
    wq_ref, wk_ref, wv_ref, wo_ref,
    emb_ref, q_ref, k_ref, v_ref, mid_ref, n2_ref,
    n1_ref,
):
    step = pl.program_id(0)

    @pl.when(step == 0)
    def _():
        inputs = (pix_ref[...] + pert_ref[...]).astype(BF16)
        embedded = mm(inputs, emb_w_ref[...])
        emb_ref[...] = embedded
        n1_ref[...] = (normalize(embedded)[0] * gain1_ref[...]).astype(BF16)
        mid_ref[...] = embedded

    n1 = n1_ref[...]
    query = mm(n1, wq_ref[...]).astype(BF16)
    keys = mm(n1, wk_ref[...]).astype(BF16)
    vals = mm(n1, wv_ref[...]).astype(BF16)
    q_ref[...] = query
    k_ref[...] = keys
    v_ref[...] = vals
    same = col_ref[...] == row_ref[...]
    width = query.shape[1]
    scale = 1.0 / math.sqrt(size)
    attended = jnp.zeros(query.shape, F32)
    for head in range(width // size):
        mask = head_mask(query.shape, head, size)
        own = jnp.where(mask, query, jnp.zeros_like(query))
        low = softmax_shares(own, keys, same, scale).astype(BF16)
        attended = jnp.where(mask, mm(low, vals), attended)
    mid_ref[...] += mm_nt(attended.astype(BF16), wo_ref[...])

    @pl.when(step == pl.num_programs(0) - 1)
    def _():
        n2_ref[...] = (normalize(mid_ref[...])[0] * gain2_ref[...]).astype(BF16)


def mlp_kernel(
    n2_ref, og_ref, mid_ref, gain_ref, up_ref, down_ref, out_ref, grad_ref, acc_out, acc_grad
):
    step = pl.program_id(0)

    @pl.when(step == 0)
    def _():
        acc_out[...] = mid_ref[...]
        acc_grad[...] = jnp.zeros_like(acc_grad)

    up = up_ref[...]
    down = down_ref[...]
    pre = mm(n2_ref[...], up)
    grad_hidden = mm(og_ref[...], down)
    root = math.sqrt(2.0 / math.pi)
    square = pre * pre
    tanh = jnp.tanh(root * pre * (1.0 + 0.044715 * square))
    half = 0.5 * (1.0 + tanh)
    act = (pre * half).astype(BF16)
    slope = half + 0.5 * pre * (1.0 - tanh * tanh) * (root * (1.0 + 3.0 * 0.044715 * square))
    grad_pre = (grad_hidden * slope).astype(BF16)
    acc_out[...] += mm_nt(act, down)
    acc_grad[...] += mm_nt(grad_pre, up)

    @pl.when(step == pl.num_programs(0) - 1)
    def _():
        out_ref[...] = acc_out[...].astype(BF16)
        grad_ref[...] = og_ref[...].astype(F32) + norm_back(
            mid_ref[...], gain_ref[...], acc_grad[...]
        )


def backward_kernel(
    size, images,
    grad_ref, emb_ref, gain_ref, emb_w_ref, pert_ref, ball_ref, col_ref, row_ref,
    q_ref, k_ref, v_ref, wq_ref, wk_ref, wv_ref, wo_ref,
    out_ref,
    low_ref, acc_ref,
):
    step = pl.program_id(0)

    @pl.when(step == 0)
    def _():
        low_ref[...] = grad_ref[...].astype(BF16)
        acc_ref[...] = jnp.zeros_like(acc_ref)

    grad_heads = mm(low_ref[...], wo_ref[...]).astype(BF16)
    query, keys, vals = q_ref[...], k_ref[...], v_ref[...]
    same = col_ref[...] == row_ref[...]
    width = query.shape[1]
    scale = 1.0 / math.sqrt(size)
    zero = jnp.zeros_like(query)
    grad_query = jnp.zeros(query.shape, F32)
    grad_keys = jnp.zeros(query.shape, F32)
    grad_vals = jnp.zeros(query.shape, F32)
    for head in range(width // size):
        mask = head_mask(query.shape, head, size)
        shares = softmax_shares(jnp.where(mask, query, zero), keys, same, scale)
        grad_shares = mm_nt(jnp.where(mask, grad_heads, zero), vals)
        grad_vals = jnp.where(mask, mm_tn(shares.astype(BF16), grad_heads), grad_vals)
        inner = jnp.sum(grad_shares * shares, -1, keepdims=True)
        grad_scores = (shares * (grad_shares - inner) * scale).astype(BF16)
        grad_query = jnp.where(mask, mm(grad_scores, keys), grad_query)
        grad_keys = jnp.where(mask, mm_tn(grad_scores, query), grad_keys)
    acc_ref[...] += (
        mm_nt(grad_query.astype(BF16), wq_ref[...])
        + mm_nt(grad_keys.astype(BF16), wk_ref[...])
        + mm_nt(grad_vals.astype(BF16), wv_ref[...])
    )

    @pl.when(step == pl.num_programs(0) - 1)
    def _():
        grad_embed = grad_ref[...] + norm_back(emb_ref[...], gain_ref[...], acc_ref[...])
        grad_input = mm_nt(grad_embed.astype(BF16), emb_w_ref[...])
        labels = col_ref[...]
        noise = pert_ref[...]
        patch = noise.shape[1]
        row_sq = jnp.sum(grad_input * grad_input, -1, keepdims=True)
        scale_rows = jnp.zeros_like(row_sq)
        counts = []
        for image in range(images):
            own = labels == image
            count = jnp.sum(jnp.where(own, 1.0, 0.0), 0, keepdims=True) * patch
            counts.append(count)
            total = jnp.sum(jnp.where(own, row_sq, 0.0), 0, keepdims=True)
            scale_rows = jnp.where(own, STEP_SIZE * lax.rsqrt(total / count + 1e-06), scale_rows)
        candidate = noise + scale_rows * grad_input
        row_sq = jnp.sum(candidate * candidate, -1, keepdims=True)
        factor_rows = jnp.zeros_like(row_sq)
        for image in range(images):
            own = labels == image
            total = jnp.sum(jnp.where(own, row_sq, 0.0), 0, keepdims=True)
            factor = jnp.minimum(
                1.0, ball_ref[:, image : image + 1] * lax.rsqrt(total / counts[image] + 1e-06)
            )
            factor_rows = jnp.where(own, factor, factor_rows)
        out_ref[...] = candidate * factor_rows


def whole(array):
    return pl.BlockSpec(array.shape, lambda j: (0,) * array.ndim)


def params():
    return pltpu.CompilerParams(
        dimension_semantics=("arbitrary",), vmem_limit_bytes=VMEM_LIMIT
    )


def body(
    pixels,
    perturbation,
    segment_ids,
    ball_radius,
    w_embed,
    gain_attn,
    w_qkv,
    w_out,
    gain_mlp,
    w_up,
    w_down,
    out_grad,
):
    rows, patch = pixels.shape
    model = w_embed.shape[1]
    chunk, _, share = w_qkv.shape
    units = w_up.shape[1]
    size = model // HEADS
    groups = model // share
    images = ball_radius.shape[1]

    mine = jnp.concatenate([w_qkv.reshape(chunk, 3 * share), w_out.T, w_up, w_down.T], 1)
    chunks = lax.all_gather(mine, "heads", axis=0, tiled=False)
    attn = chunks[:, :, : 4 * share].reshape(groups, chunk, 4, share)
    attn = attn.transpose(1, 2, 0, 3).reshape(chunk, 4 * model)
    mlp = chunks[:, :, 4 * share :].reshape(groups, chunk, 2, units)
    mlp = mlp.transpose(1, 2, 0, 3).reshape(chunk, 2 * groups * units)
    weights = lax.all_gather(jnp.concatenate([attn, mlp], 1), "rows", axis=0, tiled=True)

    labels_col = segment_ids.reshape(rows, 1)
    labels_row = segment_ids.reshape(1, rows)
    gain1 = gain_attn.reshape(1, model)
    gain2 = gain_mlp.reshape(1, model)

    quad = 4 * size
    steps = model // quad
    full = lambda dt: jax.ShapeDtypeStruct((rows, model), dt)
    block = pl.BlockSpec((rows, quad), lambda j: (0, j))
    fixed = pl.BlockSpec((rows, model), lambda j: (0, 0))
    part = lambda which: pl.BlockSpec((model, quad), lambda j: (0, which * steps + j))

    attn_in = (pixels, perturbation, w_embed, gain1, gain2, labels_col, labels_row)
    embedded, query, keys, vals, stream_mid, normed_two = pl.pallas_call(
        lambda *refs: attention_kernel(size, *refs),
        grid=(steps,),
        in_specs=[whole(a) for a in attn_in] + [part(0), part(1), part(2), part(3)],
        out_specs=[fixed, block, block, block, fixed, fixed],
        out_shape=[full(F32), full(BF16), full(BF16), full(BF16), full(F32), full(BF16)],
        scratch_shapes=[pltpu.VMEM((rows, model), BF16)],
        compiler_params=params(),
    )(*attn_in, weights, weights, weights, weights)

    width = 512
    count = groups * units // width
    first = 4 * model // width
    mlp_in = (normed_two, out_grad, stream_mid, gain2)
    block_out, grad_mid = pl.pallas_call(
        mlp_kernel,
        grid=(count,),
        in_specs=[whole(a) for a in mlp_in]
        + [
            pl.BlockSpec((model, width), lambda j: (0, first + j)),
            pl.BlockSpec((model, width), lambda j: (0, first + count + j)),
        ],
        out_specs=[fixed, fixed],
        out_shape=[full(BF16), full(F32)],
        scratch_shapes=[pltpu.VMEM((rows, model), F32), pltpu.VMEM((rows, model), F32)],
        compiler_params=params(),
    )(*mlp_in, weights, weights)

    back_in = (grad_mid, embedded, gain1, w_embed, perturbation, ball_radius, labels_col, labels_row)
    updated = pl.pallas_call(
        lambda *refs: backward_kernel(size, images, *refs),
        grid=(steps,),
        in_specs=[whole(a) for a in back_in]
        + [block, block, block, part(0), part(1), part(2), part(3)],
        out_specs=pl.BlockSpec((rows, patch), lambda j: (0, 0)),
        out_shape=jax.ShapeDtypeStruct((rows, patch), F32),
        scratch_shapes=[pltpu.VMEM((rows, model), BF16), pltpu.VMEM((rows, model), F32)],
        compiler_params=params(),
    )(*back_in, query, keys, vals, weights, weights, weights, weights)
    return (block_out, updated)


def solution(mesh):
    in_specs = (
        P("rows", None),
        P("rows", None),
        P("rows", None),
        P("rows", None),
        P(),
        P(),
        P("rows", None, "heads"),
        P("heads", "rows"),
        P(),
        P("rows", "heads"),
        P("heads", "rows"),
        P("rows", None),
    )
    out_specs = (P("rows", None), P("rows", None))
    return jax.shard_map(body, mesh=mesh, in_specs=in_specs, out_specs=out_specs, check_vma=False)
```

time: 502 us -> 209 us (0.42); the launches traced: 492 us -> 209 us
  waiting for transfers between devices: 341 us -> 110 us
  blocking collectives: 107 us -> 33.9 us
  Pallas kernels: 0 us -> 44.7 us
  matrix products: 15.9 us -> 0 us
  other arithmetic: 9.03 us -> 1.75 us
    psum x3 -> x0, waiting for transfers between devices: 341 us -> none  [the longest x1 136 us: body(): lax.psum(mlp_terms.astype(jnp.bfloat16), 'heads').astype(jnp.float32)]
    all_gather x0 -> x1, waiting for transfers between devices: none -> 110 us  [body(): lax.all_gather(jnp.concatenate([attn, mlp], 1), 'rows', axis=0, tiled=True)]
    all_gather x4 -> x1, blocking collectives: 107 us -> 33.9 us  [body(): chunks = lax.all_gather(mine, 'heads', axis=0, tiled=False)]
    pallas_call x0 -> x3, Pallas kernels: none -> 44.7 us  [the longest x1 16.9 us: body(): pl.pallas_call(lambda *refs: backward_kernel(size, images, *refs), grid=(...]
    dot_general x14 -> x0, matrix products: 15.9 us -> none  [the longest x1 3.01 us: body(): up_terms = jnp.dot(grad_pre, w_up.T, preferred_element_type=jnp.float32)]
    reduce_sum x12 -> x0, other arithmetic: 7.82 us -> none  [the longest x2 4.49 us: layer_norm(): return shifted * lax.rsqrt(spread + 1e-05) * gain]
  transfers between devices with their start and end apart: 3 -> 1, of which waited for: 3 -> 1; matrix products, arithmetic and copies ran while one was open for 0% -> 0% of each run, Pallas kernels for 0% -> 0%
where the time goes in v1:
time: 209 us
  waiting for transfers between devices  110 us (53%)
  Pallas kernels  44.7 us (21%)
  blocking collectives  33.9 us (16%)
  between operations  14.1 us (7%)
  local copies, waits for them, and re-layouts  3.87 us (2%)
    all_gather x1, waiting for transfers between devices, body(): lax.all_gather(jnp.concatenate([attn, mlp], 1), 'rows', axis=0, tiled=True)  110 us
    all_gather x1, blocking collectives, body(): chunks = lax.all_gather(mine, 'heads', axis=0, tiled=False)  33.9 us
    pallas_call x1, Pallas kernels, body(): pl.pallas_call(lambda *refs: backward_kernel(size, images, *refs), grid=(...  16.9 us
    pallas_call x1, Pallas kernels, body(): pl.pallas_call(mlp_kernel, grid=(count,), in_specs=[whole(a) for a in mlp...  15.6 us
    pallas_call x1, Pallas kernels, body(): pl.pallas_call(lambda *refs: attention_kernel(size, *refs), grid=(steps,)...  12.1 us
  transfers between devices with their start and end apart: 1, of which 1 were waited for; matrix products, arithmetic and copies ran while one was open for 0% of the time, Pallas kernels for 0%

profile of v1, /device:TPU:1, one launch (start us, length us, event | category | flops | bytes accessed | tf_op | source)
XLA Modules:
  0.0 208.5 jit_solution(2115849775013318254)
XLA Ops:
  7.2 0.0 all-gather.3.cloned.1.call-start
  7.2 0.8 copy.15
  8.0 0.1 reshape.31
  8.1 0.8 pad_maximum_fusion.1
  8.9 33.9 %all-gather = bf16[512,768]{1,0:T(8,128)(2,1)S(1)} all-gather(bf16[32,768]{1,0:T(8,128)(2,1)S(1)} %pad_maximum_fusion.1), channel_id=2, replica_groups=mesh['rows'=32,'heads'=16] {'heads'}, dimensions={0}, use_global_device_ids=true | all-gather | bytes 835584 | tf_op jit(solution)/shard_map/all_gather | solution.py:230
  42.8 0.1 reshape.34
  43.0 0.4 copy.17
  43.4 0.3 copy.20
  43.7 0.2 reshape.32
  44.0 0.6 copy.16
  44.6 0.0 copy-start
  44.6 0.5 reshape.33
  45.0 0.9 pad_maximum_fusion
  46.0 0.0 all-gather.3.cloned.1.call-update
  46.0 0.0 copy-done
  46.0 0.8 copy.18.refs_5_.refs_6_
  46.8 110.2 %all-gather.3.cloned.1.call-done.refs_7_.refs_8_.refs_9_.refs_10_.up_ref.down_ref.refs_11_.refs_12_.refs_13_.refs_14_ = bf16[1024,12288]{1,0:T(8,128)(2,1)} async-done(((bf16[32,12288]{1,0:T(8,128)(2,1)}), bf16[1024,12288]{1,0:T(8,128)(2,1)}) %all-gather.3.cloned.1.call-update) | async-done | bytes 25165840 | tf_op jit(solution)/shard_map/all_gather | solution.py:235
  157.0 12.1 %shard_map.131 = (f32[256,1024]{1,0:T(8,128)}, bf16[256,1024]{1,0:T(8,128)(2,1)}, bf16[256,1024]{1,0:T(8,128)(2,1)}, bf16[256,1024]{1,0:T(8,128)(2,1)}, f32[256,1024]{1,0:T(8,128)}, /*index=5*/bf16[256,1024]{1,0:T(8,128)(2,1)}) custom-call(f32[256,768]{1,0:T(8,128)} %refs_0_.1, f32[256,768]{1,0:T(8,128)} %refs_4_.1, bf16[768,1024]{1,0:T(8,128)(2,1)} %refs_3_.1, ...), custom_call_target="tpu_custom_call" | custom-call | tf_op jit(solution)/shard_map/pallas_call | solution.py:250
  169.1 15.6 %shard_map.132 = (bf16[256,1024]{1,0:T(8,128)(2,1)}, f32[256,1024]{1,0:T(8,128)}) custom-call(bf16[256,1024]{1,0:T(8,128)(2,1)} %get-tuple-element.10.n2_ref, bf16[256,1024]{1,0:T(8,128)(2,1)} %og_ref.1, f32[256,1024]{1,0:T(8,128)} %get-tuple-element.11.mid_ref, f32[1,1024]{1,0:T(1,128)} %bitcast.23, ...), custom_call_target="tpu_custom_call" | custom-call | tf_op jit(solution)/shard_map/pallas_call | solution.py:264
  184.7 16.9 %shard_map.133 = f32[256,768]{1,0:T(8,128)} custom-call(f32[256,1024]{1,0:T(8,128)} %get-tuple-element.13.refs_0_, f32[256,1024]{1,0:T(8,128)} %get-tuple-element.14.refs_1_, f32[1,1024]{1,0:T(1,128)} %bitcast.20, bf16[768,1024]{1,0:T(8,128)(2,1)} %refs_3_.1, f32[256,768]{1,0:T(8,128)} %refs_4_.1, f32[1,4]{1,0:T(1,128)} %refs_5_.1, ...), custom_call_target="tpu_custom_call" | custom-call | tf_op jit(solution)/shard_map/pallas_call | solution.py:279
  (2 shorter events, 0.1 us)
Async XLA Ops:
  7.2 149.8 %all-gather.3.cloned.1.call-start = ((), (), s32[]{:S(2)}) async-start(), calls=%async_computation | async-start | bytes 25952256 | tf_op jit(solution)/shard_map/all_gather | solution.py:235
  44.6 1.4 copy-start
Sparse Core Ops, SparseCore 0:
  46.1 110.8 all-gather.2

commit v2 on v1

--- a/solution.py
+++ b/solution.py
@@ -44,6 +44,12 @@
     )
 
 
+def reorder(values, perm):
+    high = values.astype(BF16)
+    rest = (values - high.astype(F32)).astype(BF16)
+    return mm_nt(high, perm) + mm_nt(rest, perm)
+
+
 def head_mask(shape, head, size):
     lane = lax.broadcasted_iota(jnp.int32, shape, 1)
     return (lane >= head * size) & (lane < (head + 1) * size)
@@ -57,10 +63,10 @@
 
 def attention_kernel(
     size,
-    pix_ref, pert_ref, emb_w_ref, gain1_ref, gain2_ref, col_ref, row_ref,
-    wq_ref, wk_ref, wv_ref, wo_ref,
+    pix_ref, pert_ref, emb_w_ref, gain1_ref, gain2_ref, col_ref, row_ref, perm_ref,
+    wq0_ref, wq1_ref, wk0_ref, wk1_ref, wv0_ref, wv1_ref, wo0_ref, wo1_ref,
     emb_ref, q_ref, k_ref, v_ref, mid_ref, n2_ref,
-    n1_ref,
+    n1_ref, acc_ref,
 ):
     step = pl.program_id(0)
 
@@ -69,13 +75,15 @@
         inputs = (pix_ref[...] + pert_ref[...]).astype(BF16)
         embedded = mm(inputs, emb_w_ref[...])
         emb_ref[...] = embedded
-        n1_ref[...] = (normalize(embedded)[0] * gain1_ref[...]).astype(BF16)
-        mid_ref[...] = embedded
-
-    n1 = n1_ref[...]
-    query = mm(n1, wq_ref[...]).astype(BF16)
-    keys = mm(n1, wk_ref[...]).astype(BF16)
-    vals = mm(n1, wv_ref[...]).astype(BF16)
+        normed = (normalize(embedded)[0] * gain1_ref[...]).astype(BF16)
+        n1_ref[...] = mm(normed, perm_ref[...]).astype(BF16)
+        acc_ref[...] = jnp.zeros_like(acc_ref)
+
+    half = n1_ref.shape[1] // 2
+    own, other = n1_ref[:, :half], n1_ref[:, half:]
+    query = (mm(own, wq0_ref[...]) + mm(other, wq1_ref[...])).astype(BF16)
+    keys = (mm(own, wk0_ref[...]) + mm(other, wk1_ref[...])).astype(BF16)
+    vals = (mm(own, wv0_ref[...]) + mm(other, wv1_ref[...])).astype(BF16)
     q_ref[...] = query
     k_ref[...] = keys
     v_ref[...] = vals
@@ -85,13 +93,16 @@
     attended = jnp.zeros(query.shape, F32)
     for head in range(width // size):
         mask = head_mask(query.shape, head, size)
-        own = jnp.where(mask, query, jnp.zeros_like(query))
-        low = softmax_shares(own, keys, same, scale).astype(BF16)
+        masked = jnp.where(mask, query, jnp.zeros_like(query))
+        low = softmax_shares(masked, keys, same, scale).astype(BF16)
         attended = jnp.where(mask, mm(low, vals), attended)
-    mid_ref[...] += mm_nt(attended.astype(BF16), wo_ref[...])
+    attended = attended.astype(BF16)
+    acc_ref[:, :half] += mm_nt(attended, wo0_ref[...])
+    acc_ref[:, half:] += mm_nt(attended, wo1_ref[...])
 
     @pl.when(step == pl.num_programs(0) - 1)
     def _():
+        mid_ref[...] = emb_ref[...] + reorder(acc_ref[...], perm_ref[...])
         n2_ref[...] = (normalize(mid_ref[...])[0] * gain2_ref[...]).astype(BF16)
 
 
@@ -129,8 +140,9 @@
 
 def backward_kernel(
     size, images,
-    grad_ref, emb_ref, gain_ref, emb_w_ref, pert_ref, ball_ref, col_ref, row_ref,
-    q_ref, k_ref, v_ref, wq_ref, wk_ref, wv_ref, wo_ref,
+    grad_ref, emb_ref, gain_ref, emb_w_ref, pert_ref, ball_ref, col_ref, row_ref, perm_ref,
+    q_ref, k_ref, v_ref,
+    wq0_ref, wq1_ref, wk0_ref, wk1_ref, wv0_ref, wv1_ref, wo0_ref, wo1_ref,
     out_ref,
     low_ref, acc_ref,
 ):
@@ -138,10 +150,12 @@
 
     @pl.when(step == 0)
     def _():
-        low_ref[...] = grad_ref[...].astype(BF16)
+        low_ref[...] = mm(grad_ref[...].astype(BF16), perm_ref[...]).astype(BF16)
         acc_ref[...] = jnp.zeros_like(acc_ref)
 
-    grad_heads = mm(low_ref[...], wo_ref[...]).astype(BF16)
+    half = low_ref.shape[1] // 2
+    grad_heads = mm(low_ref[:, :half], wo0_ref[...]) + mm(low_ref[:, half:], wo1_ref[...])
+    grad_heads = grad_heads.astype(BF16)
     query, keys, vals = q_ref[...], k_ref[...], v_ref[...]
     same = col_ref[...] == row_ref[...]
     width = query.shape[1]
@@ -159,15 +173,23 @@
         grad_scores = (shares * (grad_shares - inner) * scale).astype(BF16)
         grad_query = jnp.where(mask, mm(grad_scores, keys), grad_query)
         grad_keys = jnp.where(mask, mm_tn(grad_scores, query), grad_keys)
-    acc_ref[...] += (
-        mm_nt(grad_query.astype(BF16), wq_ref[...])
-        + mm_nt(grad_keys.astype(BF16), wk_ref[...])
-        + mm_nt(grad_vals.astype(BF16), wv_ref[...])
+    grad_query, grad_keys = grad_query.astype(BF16), grad_keys.astype(BF16)
+    grad_vals = grad_vals.astype(BF16)
+    acc_ref[:, :half] += (
+        mm_nt(grad_query, wq0_ref[...])
+        + mm_nt(grad_keys, wk0_ref[...])
+        + mm_nt(grad_vals, wv0_ref[...])
+    )
+    acc_ref[:, half:] += (
+        mm_nt(grad_query, wq1_ref[...])
+        + mm_nt(grad_keys, wk1_ref[...])
+        + mm_nt(grad_vals, wv1_ref[...])
     )
 
     @pl.when(step == pl.num_programs(0) - 1)
     def _():
-        grad_embed = grad_ref[...] + norm_back(emb_ref[...], gain_ref[...], acc_ref[...])
+        grad_norm = reorder(acc_ref[...], perm_ref[...])
+        grad_embed = grad_ref[...] + norm_back(emb_ref[...], gain_ref[...], grad_norm)
         grad_input = mm_nt(grad_embed.astype(BF16), emb_w_ref[...])
         labels = col_ref[...]
         noise = pert_ref[...]
@@ -232,7 +254,20 @@
     attn = attn.transpose(1, 2, 0, 3).reshape(chunk, 4 * model)
     mlp = chunks[:, :, 4 * share :].reshape(groups, chunk, 2, units)
     mlp = mlp.transpose(1, 2, 0, 3).reshape(chunk, 2 * groups * units)
-    weights = lax.all_gather(jnp.concatenate([attn, mlp], 1), "rows", axis=0, tiled=True)
+    weights = lax.all_gather(mlp, "rows", axis=0, tiled=True)
+
+    sites = lax.axis_size("rows") // 2
+    planes = [[2 * site + core for site in range(sites)] for core in range(2)]
+    copies = jnp.broadcast_to(attn[None], (sites,) + attn.shape)
+    near = lax.all_to_all(copies, "rows", 0, 0, axis_index_groups=planes)
+    near = near.reshape(sites * chunk, 4 * model)
+    far = lax.ppermute(near, "rows", [(row, row ^ 1) for row in range(2 * sites)])
+
+    core = lax.axis_index("rows") % 2
+    place = jnp.arange(model)
+    source = jnp.where(place < model // 2, core, 1 - core) + 2 * (place % (model // 2) // chunk)
+    source = source * chunk + place % chunk
+    perm = (place[:, None] == source[None, :]).astype(BF16)
 
     labels_col = segment_ids.reshape(rows, 1)
     labels_row = segment_ids.reshape(1, rows)
@@ -244,30 +279,30 @@
     full = lambda dt: jax.ShapeDtypeStruct((rows, model), dt)
     block = pl.BlockSpec((rows, quad), lambda j: (0, j))
     fixed = pl.BlockSpec((rows, model), lambda j: (0, 0))
-    part = lambda which: pl.BlockSpec((model, quad), lambda j: (0, which * steps + j))
-
-    attn_in = (pixels, perturbation, w_embed, gain1, gain2, labels_col, labels_row)
+    part = lambda which: pl.BlockSpec((model // 2, quad), lambda j: (0, which * steps + j))
+    parts = [part(which) for which in range(4) for _ in range(2)]
+
+    attn_in = (pixels, perturbation, w_embed, gain1, gain2, labels_col, labels_row, perm)
     embedded, query, keys, vals, stream_mid, normed_two = pl.pallas_call(
         lambda *refs: attention_kernel(size, *refs),
         grid=(steps,),
-        in_specs=[whole(a) for a in attn_in] + [part(0), part(1), part(2), part(3)],
+        in_specs=[whole(a) for a in attn_in] + parts,
         out_specs=[fixed, block, block, block, fixed, fixed],
         out_shape=[full(F32), full(BF16), full(BF16), full(BF16), full(F32), full(BF16)],
-        scratch_shapes=[pltpu.VMEM((rows, model), BF16)],
+        scratch_shapes=[pltpu.VMEM((rows, model), BF16), pltpu.VMEM((rows, model), F32)],
         compiler_params=params(),
-    )(*attn_in, weights, weights, weights, weights)
+    )(*attn_in, *[near, far] * 4)
 
     width = 512
     count = groups * units // width
-    first = 4 * model // width
     mlp_in = (normed_two, out_grad, stream_mid, gain2)
     block_out, grad_mid = pl.pallas_call(
         mlp_kernel,
         grid=(count,),
         in_specs=[whole(a) for a in mlp_in]
         + [
-            pl.BlockSpec((model, width), lambda j: (0, first + j)),
-            pl.BlockSpec((model, width), lambda j: (0, first + count + j)),
+            pl.BlockSpec((model, width), lambda j: (0, j)),
+            pl.BlockSpec((model, width), lambda j: (0, count + j)),
         ],
         out_specs=[fixed, fixed],
         out_shape=[full(BF16), full(F32)],
@@ -275,17 +310,19 @@
         compiler_params=params(),
     )(*mlp_in, weights, weights)
 
-    back_in = (grad_mid, embedded, gain1, w_embed, perturbation, ball_radius, labels_col, labels_row)
+    back_in = (grad_mid, embedded, gain1, w_embed, perturbation, ball_radius)
+    back_in = back_in + (labels_col, labels_row, perm)
     updated = pl.pallas_call(
         lambda *refs: backward_kernel(size, images, *refs),
         grid=(steps,),
         in_specs=[whole(a) for a in back_in]
-        + [block, block, block, part(0), part(1), part(2), part(3)],
+        + [block, block, block]
+        + parts,
         out_specs=pl.BlockSpec((rows, patch), lambda j: (0, 0)),
         out_shape=jax.ShapeDtypeStruct((rows, patch), F32),
         scratch_shapes=[pltpu.VMEM((rows, model), BF16), pltpu.VMEM((rows, model), F32)],
         compiler_params=params(),
-    )(*back_in, query, keys, vals, weights, weights, weights, weights)
+    )(*back_in, query, keys, vals, *[near, far] * 4)
     return (block_out, updated)
 
 

time: 209 us -> 200 us (0.957)
  waiting for transfers between devices: 110 us -> 23 us
  blocking collectives: 33.9 us -> 92.8 us
  starting transfers between devices: 0.04 us -> 10.9 us
  Pallas kernels: 44.7 us -> 50.4 us
    all_gather x1, waiting for transfers between devices: 110 us -> 19.2 us  [body(): weights = lax.all_gather(mlp, 'rows', axis=0, tiled=True)]
    all_to_all x0 -> x1, blocking collectives: none -> 58.9 us  [body(): near = lax.all_to_all(copies, 'rows', 0, 0, axis_index_groups=planes)]
    ppermute x0 -> x1, starting transfers between devices: none -> 10.9 us  [body(): lax.ppermute(near, 'rows', [(row, row ^ 1) for row in range(2 * sites)])]
    ppermute x0 -> x1, waiting for transfers between devices: none -> 3.79 us  [body(): lax.ppermute(near, 'rows', [(row, row ^ 1) for row in range(2 * sites)])]
    pallas_call x1, Pallas kernels: 12.1 us -> 15.2 us  [body(): pl.pallas_call(lambda *refs: attention_kernel(size, *refs), grid=(steps,)...]
    pallas_call x1, Pallas kernels: 16.9 us -> 19.6 us  [body(): pl.pallas_call(lambda *refs: backward_kernel(size, images, *refs), grid=(...]
    convert_element_type x0 -> x1, other arithmetic: none -> 2.29 us  [body(): perm = (place[:, None] == source[None, :]).astype(BF16)]
  transfers between devices with their start and end apart: 1 -> 2, of which waited for: 1 -> 2; matrix products, arithmetic and copies ran while one was open for 0% -> 2% of each run, Pallas kernels for 0% -> 8%
where the time goes in v2:
time: 200 us
  blocking collectives  92.8 us (46%)
  Pallas kernels  50.4 us (25%)
  waiting for transfers between devices  23 us (12%)
  between operations  14.1 us (7%)
  starting transfers between devices  10.9 us (5%)
  local copies, waits for them, and re-layouts  5.18 us (3%)
  other arithmetic  3.12 us (2%)
    all_to_all x1, blocking collectives, body(): near = lax.all_to_all(copies, 'rows', 0, 0, axis_index_groups=planes)  58.9 us
    all_gather x1, blocking collectives, body(): chunks = lax.all_gather(mine, 'heads', axis=0, tiled=False)  33.9 us
    pallas_call x1, Pallas kernels, body(): pl.pallas_call(lambda *refs: backward_kernel(size, images, *refs), grid=(...  19.6 us
    all_gather x1, waiting for transfers between devices, body(): weights = lax.all_gather(mlp, 'rows', axis=0, tiled=True)  19.2 us
    pallas_call x1, Pallas kernels, body(): pl.pallas_call(mlp_kernel, grid=(count,), in_specs=[whole(a) for a in mlp...  15.6 us
    pallas_call x1, Pallas kernels, body(): pl.pallas_call(lambda *refs: attention_kernel(size, *refs), grid=(steps,)...  15.2 us
    ppermute x1, starting transfers between devices, body(): lax.ppermute(near, 'rows', [(row, row ^ 1) for row in range(2 * sites)])  10.9 us
  transfers between devices with their start and end apart: 2, of which 2 were waited for; matrix products, arithmetic and copies ran while one was open for 2% of the time, Pallas kernels for 8%

profile of v2, /device:TPU:1, one launch (start us, length us, event | category | flops | bytes accessed | tf_op | source)
XLA Modules:
  0.0 199.6 jit_solution(2835804517557353737)
XLA Ops:
  7.2 0.0 all-gather.3.cloned.1.call-start
  7.2 0.8 copy.20
  8.0 0.1 reshape.70
  8.1 0.8 pad_maximum_fusion
  8.9 33.9 %all-gather = bf16[512,768]{1,0:T(8,128)(2,1)S(1)} all-gather(bf16[32,768]{1,0:T(8,128)(2,1)S(1)} %pad_maximum_fusion), channel_id=2, replica_groups=mesh['rows'=32,'heads'=16] {'heads'}, dimensions={0}, use_global_device_ids=true | all-gather | bytes 835584 | tf_op jit(solution)/shard_map/all_gather | solution.py:252
  42.8 0.1 reshape.73
  42.9 0.4 copy.23
  43.4 1.1 copy.25
  44.5 0.0 all-gather.3.cloned.1.call-update
  44.5 0.2 reshape.71
  44.8 0.6 copy.27
  45.4 0.5 broadcast_in_dim.19
  45.8 0.5 broadcast_in_dim.20
  46.4 0.0 copy-start
  46.4 58.9 %all_to_all.5 = bf16[16,32,4096]{2,1,0:T(8,128)(2,1)} all-to-all(bf16[16,32,4096]{2,1,0:T(8,128)(2,1)S(1)} %broadcast_in_dim.20), channel_id=1, replica_groups={{0,32,64,96,128,160,192,224,256,288,320,352,384,416,448,480},{16,48,80,..., dimensions={0} | all-to-all | bytes 8388608 | tf_op jit(solution)/shard_map/all_to_all | solution.py:262
  105.3 10.9 %collective-permute-start = (bf16[512,4096]{1,0:T(8,128)(2,1)}, bf16[512,4096]{1,0:T(8,128)(2,1)}, u32[]{:S(2)}, u32[]{:S(2)}) collective-permute-start(bf16[512,4096]{1,0:T(8,128)(2,1)} %bitcast.7.refs_8_.refs_10_.refs_12_.refs_14_.refs_16_.refs_18_), channel_id=1, source_target_pairs={{0,16},{16,0},{32,48},{48,32},{64,80},{80,64},{96,112},{112,96},{1... | collective-permute-start | bytes 12582920 | tf_op jit(solution)/shard_map/ppermute | solution.py:264
  116.2 0.0 copy-done
  116.2 0.8 copy.22.refs_5_.refs_6_
  117.0 2.3 %fusion.refs_7_.refs_8_ = bf16[1024,1024]{1,0:T(8,128)(2,1)} fusion(s32[1024]{0:T(1024)S(1)} %fusion.5), kind=kLoop, calls=%fused_computation.1 | loop fusion | flops 2097152 | bytes 2101248 | tf_op jit(solution)/shard_map/convert_element_type | solution.py:270
  119.3 3.8 %collective-permute-done.refs_9_.refs_11_.refs_13_.refs_15_.refs_17_.refs_19_ = bf16[512,4096]{1,0:T(8,128)(2,1)} collective-permute-done((bf16[512,4096]{1,0:T(8,128)(2,1)}, bf16[512,4096]{1,0:T(8,128)(2,1)}, u32[]{:S(2)}, u32[]{:S(2)}) %collective-permute-start) | collective-permute-done | bytes 4194336 | tf_op jit(solution)/shard_map/ppermute | solution.py:264
  123.1 15.2 %shard_map.131 = (f32[256,1024]{1,0:T(8,128)}, bf16[256,1024]{1,0:T(8,128)(2,1)}, bf16[256,1024]{1,0:T(8,128)(2,1)}, bf16[256,1024]{1,0:T(8,128)(2,1)}, f32[256,1024]{1,0:T(8,128)}, /*index=5*/bf16[256,1024]{1,0:T(8,128)(2,1)}) custom-call(f32[256,768]{1,0:T(8,128)} %refs_0_.1, f32[256,768]{1,0:T(8,128)} %refs_4_.1, bf16[768,1024]{1,0:T(8,128)(2,1)} %refs_3_.1, ...), custom_call_target="tpu_custom_call" | custom-call | tf_op jit(solution)/shard_map/pallas_call | solution.py:286
  138.3 19.2 %all-gather.3.cloned.1.call-done.up_ref.down_ref = bf16[1024,8192]{1,0:T(8,128)(2,1)} async-done(((bf16[32,8192]{1,0:T(8,128)(2,1)}), bf16[1024,8192]{1,0:T(8,128)(2,1)}) %all-gather.3.cloned.1.call-update) | async-done | bytes 16777232 | tf_op jit(solution)/shard_map/all_gather | solution.py:257
  157.5 15.6 %shard_map.132 = (bf16[256,1024]{1,0:T(8,128)(2,1)}, f32[256,1024]{1,0:T(8,128)}) custom-call(bf16[256,1024]{1,0:T(8,128)(2,1)} %get-tuple-element.10.n2_ref, bf16[256,1024]{1,0:T(8,128)(2,1)} %og_ref.1, f32[256,1024]{1,0:T(8,128)} %get-tuple-element.11.mid_ref, f32[1,1024]{1,0:T(1,128)} %bitcast.23, ...), custom_call_target="tpu_custom_call" | custom-call | tf_op jit(solution)/shard_map/pallas_call | solution.py:299
  173.1 19.6 %shard_map.133 = f32[256,768]{1,0:T(8,128)} custom-call(f32[256,1024]{1,0:T(8,128)} %get-tuple-element.13.refs_0_, f32[256,1024]{1,0:T(8,128)} %get-tuple-element.14.refs_1_, f32[1,1024]{1,0:T(1,128)} %bitcast.26, bf16[768,1024]{1,0:T(8,128)(2,1)} %refs_3_.1, f32[256,768]{1,0:T(8,128)} %refs_4_.1, f32[1,4]{1,0:T(1,128)} %refs_5_.1, ...), custom_call_target="tpu_custom_call" | custom-call | tf_op jit(solution)/shard_map/pallas_call | solution.py:315
  (3 shorter events, 0.1 us)
Async XLA Ops:
  7.2 150.3 %all-gather.3.cloned.1.call-start = ((), (), s32[]{:S(2)}) async-start(), calls=%async_computation.1 | async-start | bytes 17301504 | tf_op jit(solution)/shard_map/all_gather | solution.py:257
  46.4 69.8 %copy-start = (s32[1,256]{1,0:T(1,128)S(1)}, s32[1,256]{1,0:T(1,128)}, u32[]{:S(2)}) copy-start(s32[1,256]{1,0:T(1,128)} %refs_7_.1) | copy-start | bytes 3076
  105.3 17.8 %collective-permute-start = (bf16[512,4096]{1,0:T(8,128)(2,1)}, bf16[512,4096]{1,0:T(8,128)(2,1)}, u32[]{:S(2)}, u32[]{:S(2)}) collective-permute-start(bf16[512,4096]{1,0:T(8,128)(2,1)} %bitcast.7.refs_8_.refs_10_.refs_12_.refs_14_.refs_16_.refs_18_), channel_id=1, source_target_pairs={{0,16},{16,0},{32,48},{48,32},{64,80},{80,64},{96,112},{112,96},{1... | collective-permute-start | bytes 12582920 | tf_op jit(solution)/shard_map/ppermute | solution.py:264
Sparse Core Ops, SparseCore 0:
  44.6 112.8 all-gather.2

commit v3 on v2

v3 whole, which is shorter than its diff:
```python
import math

import jax
import jax.numpy as jnp
from jax import lax
from jax.experimental import pallas as pl
from jax.experimental.pallas import tpu as pltpu
from jax.sharding import PartitionSpec as P

HEADS = 16
STEP_SIZE = 0.1
VMEM_LIMIT = 56 * 1024 * 1024
F32 = jnp.float32
BF16 = jnp.bfloat16


def mm(a, b):
    return lax.dot_general(a, b, (((1,), (0,)), ((), ())), preferred_element_type=F32)


def mm_nt(a, b):
    return lax.dot_general(a, b, (((1,), (1,)), ((), ())), preferred_element_type=F32)


def mm_tn(a, b):
    return lax.dot_general(a, b, (((0,), (0,)), ((), ())), preferred_element_type=F32)


def normalize(values):
    center = jnp.mean(values, -1, keepdims=True)
    shifted = values - center
    spread = jnp.mean(shifted * shifted, -1, keepdims=True)
    inv = lax.rsqrt(spread + 1e-05)
    return shifted * inv, inv


def norm_back(values, gain, upstream):
    hat, inv = normalize(values)
    scaled = upstream * gain
    return inv * (
        scaled
        - jnp.mean(scaled, -1, keepdims=True)
        - hat * jnp.mean(scaled * hat, -1, keepdims=True)
    )


def reorder(values, perm):
    high = values.astype(BF16)
    rest = (values - high.astype(F32)).astype(BF16)
    return mm_nt(high, perm) + mm_nt(rest, perm)


def head_mask(shape, head, size):
    lane = lax.broadcasted_iota(jnp.int32, shape, 1)
    return (lane >= head * size) & (lane < (head + 1) * size)


def softmax_shares(query, keys, same, scale):
    scores = mm_nt(query, keys) * scale
    powers = jnp.where(same, jnp.exp(scores), 0.0)
    return powers * (1.0 / jnp.sum(powers, -1, keepdims=True))


def attention_kernel(
    size,
    pix_ref, pert_ref, emb_w_ref, gain1_ref, gain2_ref, col_ref, row_ref, perm_ref,
    wq0_ref, wq1_ref, wk0_ref, wk1_ref, wv0_ref, wv1_ref, wo0_ref, wo1_ref,
    emb_ref, q_ref, k_ref, v_ref, mid_ref, n2_ref, low_ref, turned_ref,
    n1_ref, acc_ref,
):
    step = pl.program_id(0)

    @pl.when(step == 0)
    def _():
        inputs = (pix_ref[...] + pert_ref[...]).astype(BF16)
        embedded = mm(inputs, emb_w_ref[...])
        emb_ref[...] = embedded
        normed = (normalize(embedded)[0] * gain1_ref[...]).astype(BF16)
        n1_ref[...] = mm(normed, perm_ref[...]).astype(BF16)
        acc_ref[...] = jnp.zeros_like(acc_ref)

    half = n1_ref.shape[1] // 2
    own, other = n1_ref[:, :half], n1_ref[:, half:]
    query = (mm(own, wq0_ref[...]) + mm(other, wq1_ref[...])).astype(BF16)
    keys = (mm(own, wk0_ref[...]) + mm(other, wk1_ref[...])).astype(BF16)
    vals = (mm(own, wv0_ref[...]) + mm(other, wv1_ref[...])).astype(BF16)
    q_ref[...] = query
    k_ref[...] = keys
    v_ref[...] = vals
    same = col_ref[...] == row_ref[...]
    width = query.shape[1]
    scale = 1.0 / math.sqrt(size)
    attended = jnp.zeros(query.shape, F32)
    for head in range(width // size):
        mask = head_mask(query.shape, head, size)
        masked = jnp.where(mask, query, jnp.zeros_like(query))
        shares = softmax_shares(masked, keys, same, scale)
        low = shares.astype(BF16)
        low_ref[head] = low
        turned_ref[head] = shares.T.astype(BF16)
        attended = jnp.where(mask, mm(low, vals), attended)
    attended = attended.astype(BF16)
    acc_ref[:, :half] += mm_nt(attended, wo0_ref[...])
    acc_ref[:, half:] += mm_nt(attended, wo1_ref[...])

    @pl.when(step == pl.num_programs(0) - 1)
    def _():
        mid_ref[...] = emb_ref[...] + reorder(acc_ref[...], perm_ref[...])
        n2_ref[...] = (normalize(mid_ref[...])[0] * gain2_ref[...]).astype(BF16)


def tail_kernel(
    size, images,
    n2_hbm, og_hbm, mid_hbm, weights_hbm, near_hbm, far_hbm, q_hbm, k_hbm, v_hbm,
    low_hbm, turned_hbm, emb_hbm, emb_w_hbm, pert_hbm,
    gain1_ref, gain2_ref, ball_ref, col_ref,
    out_ref, new_ref,
    n2_ref, og_ref, mid_ref, up_buf, down_buf, attn_buf, qkv_buf,
    low_buf, turned_buf, emb_ref, emb_w_ref, pert_ref,
    acc_out, acc_grad, heads_ref, proj_ref,
    up_sem, down_sem, sem,
):
    rows, model = n2_ref.shape
    chunks, _, width = up_buf.shape
    core = lax.rem(lax.axis_index("rows"), 2)

    def up_copy(j):
        start = pl.multiple_of(j * width, width)
        source = weights_hbm.at[:, pl.ds(start, width)]
        return pltpu.make_async_copy(source, up_buf.at[j], up_sem.at[j])

    def down_copy(j):
        start = pl.multiple_of((chunks + j) * width, width)
        source = weights_hbm.at[:, pl.ds(start, width)]
        return pltpu.make_async_copy(source, down_buf.at[j], down_sem.at[j])

    pairs = (
        (n2_hbm, n2_ref),
        (og_hbm, og_ref),
        (mid_hbm, mid_ref),
        (near_hbm, attn_buf.at[:, core]),
        (far_hbm, attn_buf.at[:, 1 - core]),
        (q_hbm, qkv_buf.at[0]),
        (k_hbm, qkv_buf.at[1]),
        (v_hbm, qkv_buf.at[2]),
        (low_hbm, low_buf),
        (turned_hbm, turned_buf),
        (emb_hbm, emb_ref),
        (emb_w_hbm, emb_w_ref),
        (pert_hbm, pert_ref),
    )
    copies = [pltpu.make_async_copy(*pair, sem.at[i]) for i, pair in enumerate(pairs)]

    copies[0].start()
    up_copy(0).start()
    copies[1].start()
    down_copy(0).start()
    copies[2].start()
    up_copy(1).start()
    down_copy(1).start()
    acc_out[...] = jnp.zeros_like(acc_out)
    acc_grad[...] = jnp.zeros_like(acc_grad)
    for copy in copies[:2]:
        copy.wait()

    def mlp_step(j, carry):
        @pl.when(j + 2 < chunks)
        def _():
            up_copy(j + 2).start()
            down_copy(j + 2).start()

        @pl.when(j + 2 == chunks)
        def _():
            for copy in copies[3:]:
                copy.start()

        up_copy(j).wait()
        pre = mm(n2_ref[...], up_buf[j])
        down_copy(j).wait()
        grad_hidden = mm(og_ref[...], down_buf[j])
        root = math.sqrt(2.0 / math.pi)
        square = pre * pre
        tanh = jnp.tanh(root * pre * (1.0 + 0.044715 * square))
        half = 0.5 * (1.0 + tanh)
        act = (pre * half).astype(BF16)
        slope = half + 0.5 * pre * (1.0 - tanh * tanh) * (root * (1.0 + 3.0 * 0.044715 * square))
        grad_pre = (grad_hidden * slope).astype(BF16)
        acc_out[...] += mm_nt(act, down_buf[j])
        acc_grad[...] += mm_nt(grad_pre, up_buf[j])
        return carry

    lax.fori_loop(0, chunks, mlp_step, 0)
    copies[2].wait()
    out_ref[...] = (mid_ref[...] + acc_out[...]).astype(BF16)
    grad_mid = og_ref[...].astype(F32) + norm_back(mid_ref[...], gain2_ref[...], acc_grad[...])
    acc_grad[...] = grad_mid
    for copy in copies[3:]:
        copy.wait()

    def weights(first, last):
        return attn_buf[:, :, :, first * model : last * model].reshape(
            model, (last - first) * model
        )

    heads_ref[...] = mm(grad_mid.astype(BF16), weights(3, 4)).astype(BF16)
    quad = 4 * size
    scale = 1.0 / math.sqrt(size)

    def attention_step(j, carry):
        lanes = pl.ds(pl.multiple_of(j * quad, quad), quad)
        query, keys, vals = qkv_buf[0, :, lanes], qkv_buf[1, :, lanes], qkv_buf[2, :, lanes]
        grad_heads = heads_ref[:, lanes]
        zero = jnp.zeros_like(grad_heads)
        grad_query = jnp.zeros((rows, quad), F32)
        grad_keys = jnp.zeros((rows, quad), F32)
        grad_vals = jnp.zeros((rows, quad), F32)
        for head in range(4):
            mask = head_mask((rows, quad), head, size)
            shares = low_buf[j * 4 + head].astype(F32)
            grad_shares = mm_nt(jnp.where(mask, grad_heads, zero), vals)
            grad_vals = jnp.where(mask, mm(turned_buf[j * 4 + head], grad_heads), grad_vals)
            inner = jnp.sum(grad_shares * shares, -1, keepdims=True)
            grad_scores = (shares * (grad_shares - inner) * scale).astype(BF16)
            grad_query = jnp.where(mask, mm(grad_scores, keys), grad_query)
            grad_keys = jnp.where(mask, mm_tn(grad_scores, query), grad_keys)
        for which, value in enumerate((grad_query, grad_keys, grad_vals)):
            start = pl.multiple_of(which * model + j * quad, quad)
            proj_ref[:, pl.ds(start, quad)] = value.astype(BF16)
        return carry

    lax.fori_loop(0, model // quad, attention_step, 0)
    grad_norm = mm_nt(proj_ref[...], weights(0, 3))
    grad_embed = acc_grad[...] + norm_back(emb_ref[...], gain1_ref[...], grad_norm)
    grad_input = mm_nt(grad_embed.astype(BF16), emb_w_ref[...])
    labels = col_ref[...]
    noise = pert_ref[...]
    patch = noise.shape[1]
    row_sq = jnp.sum(grad_input * grad_input, -1, keepdims=True)
    scale_rows = jnp.zeros_like(row_sq)
    counts = []
    for image in range(images):
        own = labels == image
        count = jnp.sum(jnp.where(own, 1.0, 0.0), 0, keepdims=True) * patch
        counts.append(count)
        total = jnp.sum(jnp.where(own, row_sq, 0.0), 0, keepdims=True)
        scale_rows = jnp.where(own, STEP_SIZE * lax.rsqrt(total / count + 1e-06), scale_rows)
    candidate = noise + scale_rows * grad_input
    row_sq = jnp.sum(candidate * candidate, -1, keepdims=True)
    factor_rows = jnp.zeros_like(row_sq)
    for image in range(images):
        own = labels == image
        total = jnp.sum(jnp.where(own, row_sq, 0.0), 0, keepdims=True)
        factor = jnp.minimum(
            1.0, ball_ref[:, image : image + 1] * lax.rsqrt(total / counts[image] + 1e-06)
        )
        factor_rows = jnp.where(own, factor, factor_rows)
    new_ref[...] = candidate * factor_rows


def whole(array):
    return pl.BlockSpec(array.shape, lambda j: (0,) * array.ndim)


def params():
    return pltpu.CompilerParams(
        dimension_semantics=("arbitrary",), vmem_limit_bytes=VMEM_LIMIT
    )


def body(
    pixels,
    perturbation,
    segment_ids,
    ball_radius,
    w_embed,
    gain_attn,
    w_qkv,
    w_out,
    gain_mlp,
    w_up,
    w_down,
    out_grad,
):
    rows, patch = pixels.shape
    model = w_embed.shape[1]
    chunk, _, share = w_qkv.shape
    units = w_up.shape[1]
    size = model // HEADS
    groups = model // share
    images = ball_radius.shape[1]

    mine = jnp.concatenate([w_qkv.reshape(chunk, 3 * share), w_out.T, w_up, w_down.T], 1)
    chunks = lax.all_gather(mine, "heads", axis=0, tiled=False)
    attn = chunks[:, :, : 4 * share].reshape(groups, chunk, 4, share)
    attn = attn.transpose(1, 2, 0, 3).reshape(chunk, 4 * model)
    mlp = chunks[:, :, 4 * share :].reshape(groups, chunk, 2, units)
    mlp = mlp.transpose(1, 2, 0, 3).reshape(chunk, 2 * groups * units)
    weights = lax.all_gather(mlp, "rows", axis=0, tiled=True)

    sites = lax.axis_size("rows") // 2
    planes = [[2 * site + core for site in range(sites)] for core in range(2)]
    copies = jnp.broadcast_to(attn[None], (sites,) + attn.shape)
    near = lax.all_to_all(copies, "rows", 0, 0, axis_index_groups=planes)
    near = near.reshape(sites * chunk, 4 * model)
    far = lax.ppermute(near, "rows", [(row, row ^ 1) for row in range(2 * sites)])

    core = lax.axis_index("rows") % 2
    place = jnp.arange(model)
    source = jnp.where(place < model // 2, core, 1 - core) + 2 * (place % (model // 2) // chunk)
    source = source * chunk + place % chunk
    perm = (place[:, None] == source[None, :]).astype(BF16)

    labels_col = segment_ids.reshape(rows, 1)
    labels_row = segment_ids.reshape(1, rows)
    gain1 = gain_attn.reshape(1, model)
    gain2 = gain_mlp.reshape(1, model)

    quad = 4 * size
    steps = model // quad
    full = lambda dt: jax.ShapeDtypeStruct((rows, model), dt)
    block = pl.BlockSpec((rows, quad), lambda j: (0, j))
    square = pl.BlockSpec((4, rows, rows), lambda j: (j, 0, 0))
    fixed = pl.BlockSpec((rows, model), lambda j: (0, 0))
    part = lambda which: pl.BlockSpec((model // 2, quad), lambda j: (0, which * steps + j))
    parts = [part(which) for which in range(4) for _ in range(2)]

    attn_in = (pixels, perturbation, w_embed, gain1, gain2, labels_col, labels_row, perm)
    embedded, query, keys, vals, stream_mid, normed_two, low, turned = pl.pallas_call(
        lambda *refs: attention_kernel(size, *refs),
        grid=(steps,),
        in_specs=[whole(a) for a in attn_in] + parts,
        out_specs=[fixed, block, block, block, fixed, fixed, square, square],
        out_shape=[full(F32), full(BF16), full(BF16), full(BF16), full(F32), full(BF16)]
        + [jax.ShapeDtypeStruct((HEADS, rows, rows), BF16)] * 2,
        scratch_shapes=[pltpu.VMEM((rows, model), BF16), pltpu.VMEM((rows, model), F32)],
        compiler_params=params(),
    )(*attn_in, *[near, far] * 4)

    width = 1024
    count = groups * units // width
    shard = (sites, chunk, 4 * model)
    moved = (normed_two, out_grad, stream_mid, weights, near.reshape(shard), far.reshape(shard))
    moved = moved + (query, keys, vals, low, turned, embedded, w_embed, perturbation)
    kept = (gain1, gain2, ball_radius, labels_col)
    vmem = pl.BlockSpec(memory_space=pltpu.VMEM)
    block_out, updated = pl.pallas_call(
        lambda *refs: tail_kernel(size, images, *refs),
        in_specs=[pl.BlockSpec(memory_space=pl.ANY)] * len(moved) + [vmem] * len(kept),
        out_specs=[vmem, vmem],
        out_shape=[full(BF16), jax.ShapeDtypeStruct((rows, patch), F32)],
        scratch_shapes=[
            pltpu.VMEM((rows, model), BF16),
            pltpu.VMEM((rows, model), BF16),
            pltpu.VMEM((rows, model), F32),
            pltpu.VMEM((count, model, width), BF16),
            pltpu.VMEM((count, model, width), BF16),
            pltpu.VMEM((sites, 2, chunk, 4 * model), BF16),
            pltpu.VMEM((3, rows, model), BF16),
            pltpu.VMEM((HEADS, rows, rows), BF16),
            pltpu.VMEM((HEADS, rows, rows), BF16),
            pltpu.VMEM((rows, model), F32),
            pltpu.VMEM((patch, model), BF16),
            pltpu.VMEM((rows, patch), F32),
            pltpu.VMEM((rows, model), F32),
            pltpu.VMEM((rows, model), F32),
            pltpu.VMEM((rows, model), BF16),
            pltpu.VMEM((rows, 3 * model), BF16),
            pltpu.SemaphoreType.DMA((count,)),
            pltpu.SemaphoreType.DMA((count,)),
            pltpu.SemaphoreType.DMA((13,)),
        ],
        compiler_params=pltpu.CompilerParams(vmem_limit_bytes=VMEM_LIMIT),
    )(*moved, *kept)
    return (block_out, updated)


def solution(mesh):
    in_specs = (
        P("rows", None),
        P("rows", None),
        P("rows", None),
        P("rows", None),
        P(),
        P(),
        P("rows", None, "heads"),
        P("heads", "rows"),
        P(),
        P("rows", "heads"),
        P("heads", "rows"),
        P("rows", None),
    )
    out_specs = (P("rows", None), P("rows", None))
    return jax.shard_map(body, mesh=mesh, in_specs=in_specs, out_specs=out_specs, check_vma=False)
```

time: 200 us -> 190 us (0.950)
  Pallas kernels: 50.4 us -> 41.3 us
    pallas_call x2 -> x1, Pallas kernels: 35.2 us -> 25 us  [body(): pl.pallas_call(lambda *refs: tail_kernel(size, images, *refs), in_specs=[...]
  transfers between devices with their start and end apart: 2 -> 2, of which waited for: 2 -> 2; matrix products, arithmetic and copies ran while one was open for 2% -> 3% of each run, Pallas kernels for 8% -> 9%
where the time goes in v3:
time: 190 us; the launch traced here: 189 us
  blocking collectives  92.8 us (49%)
  Pallas kernels  41.3 us (22%)
  waiting for transfers between devices  22.1 us (12%)
  between operations  14.1 us (7%)
  starting transfers between devices  10.8 us (6%)
  local copies, waits for them, and re-layouts  5.18 us (3%)
  other arithmetic  3.12 us (2%)
    all_to_all x1, blocking collectives, body(): near = lax.all_to_all(copies, 'rows', 0, 0, axis_index_groups=planes)  58.9 us
    all_gather x1, blocking collectives, body(): chunks = lax.all_gather(mine, 'heads', axis=0, tiled=False)  33.9 us
    pallas_call x1, Pallas kernels, body(): pl.pallas_call(lambda *refs: tail_kernel(size, images, *refs), in_specs=[...  25 us
    all_gather x1, waiting for transfers between devices, body(): weights = lax.all_gather(mlp, 'rows', axis=0, tiled=True)  18.1 us
    pallas_call x1, Pallas kernels, body(): pl.pallas_call(lambda *refs: attention_kernel(size, *refs), grid=(steps,)...  16.3 us
    ppermute x1, starting transfers between devices, body(): lax.ppermute(near, 'rows', [(row, row ^ 1) for row in range(2 * sites)])  10.7 us
    ppermute x1, waiting for transfers between devices, body(): lax.ppermute(near, 'rows', [(row, row ^ 1) for row in range(2 * sites)])  3.98 us
  transfers between devices with their start and end apart: 2, of which 2 were waited for; matrix products, arithmetic and copies ran while one was open for 3% of the time, Pallas kernels for 9%

profile of v3, /device:TPU:1, one launch (start us, length us, event | category | flops | bytes accessed | tf_op | source)
XLA Modules:
  0.0 189.4 jit_solution(13318412252996530514)
XLA Ops:
  7.2 0.0 all-gather.3.cloned.1.call-start
  7.2 0.8 copy.16
  8.0 0.1 reshape.73
  8.1 0.8 pad_maximum_fusion
  8.9 33.9 %all-gather = bf16[512,768]{1,0:T(8,128)(2,1)S(1)} all-gather(bf16[32,768]{1,0:T(8,128)(2,1)S(1)} %pad_maximum_fusion), channel_id=2, replica_groups=mesh['rows'=32,'heads'=16] {'heads'}, dimensions={0}, use_global_device_ids=true | all-gather | bytes 835584 | tf_op jit(solution)/shard_map/all_gather | solution.py:293
  42.8 0.1 reshape.76
  42.9 0.4 copy.19
  43.4 1.1 copy.21
  44.5 0.0 all-gather.3.cloned.1.call-update
  44.5 0.2 reshape.74
  44.8 0.6 copy.17
  45.4 0.5 broadcast_in_dim.19
  45.8 0.5 broadcast_in_dim.20
  46.4 0.0 copy-start
  46.4 58.9 %all_to_all.5.refs_4_ = bf16[16,32,4096]{2,1,0:T(8,128)(2,1)} all-to-all(bf16[16,32,4096]{2,1,0:T(8,128)(2,1)S(1)} %broadcast_in_dim.20), channel_id=1, replica_groups={{0,32,64,96,128,160,192,224,256,288,320,352,384,416,448,480},{16,48,80,..., dimensions={0} | all-to-all | bytes 8388608 | tf_op jit(solution)/shard_map/all_to_all | solution.py:303
  105.3 10.7 %collective-permute-start = (bf16[512,4096]{1,0:T(8,128)(2,1)}, bf16[512,4096]{1,0:T(8,128)(2,1)}, u32[]{:S(2)}, u32[]{:S(2)}) collective-permute-start(bf16[512,4096]{1,0:T(8,128)(2,1)} %bitcast.7.refs_8_.refs_10_.refs_12_.refs_14_), channel_id=1, source_target_pairs={{0,16},{16,0},{32,48},{48,32},{64,80},{80,64},{96,112},{112,96},{1... | collective-permute-start | bytes 12582920 | tf_op jit(solution)/shard_map/ppermute | solution.py:305
  116.0 0.0 copy-done
  116.0 0.8 copy.18.refs_5_.refs_17_
  116.8 2.3 %fusion.refs_7_ = bf16[1024,1024]{1,0:T(8,128)(2,1)} fusion(s32[1024]{0:T(1024)S(1)} %fusion.5), kind=kLoop, calls=%fused_computation.1 | loop fusion | flops 2097152 | bytes 2101248 | tf_op jit(solution)/shard_map/convert_element_type | solution.py:311
  119.1 4.0 %collective-permute-done.refs_9_.refs_11_.refs_13_.refs_15_ = bf16[512,4096]{1,0:T(8,128)(2,1)} collective-permute-done((bf16[512,4096]{1,0:T(8,128)(2,1)}, bf16[512,4096]{1,0:T(8,128)(2,1)}, u32[]{:S(2)}, u32[]{:S(2)}) %collective-permute-start) | collective-permute-done | bytes 4194336 | tf_op jit(solution)/shard_map/ppermute | solution.py:305
  123.1 16.3 %shard_map.131 = (f32[256,1024]{1,0:T(8,128)}, bf16[256,1024]{1,0:T(8,128)(2,1)}, bf16[256,1024]{1,0:T(8,128)(2,1)}, bf16[256,1024]{1,0:T(8,128)(2,1)}, f32[256,...) custom-call(f32[256,768]{1,0:T(8,128)} %refs_0_.1, ...), custom_call_target="tpu_custom_call" | custom-call | tf_op jit(solution)/shard_map/pallas_call | solution.py:328
  139.4 18.1 %all-gather.3.cloned.1.call-done.refs_3_ = bf16[1024,8192]{1,0:T(8,128)(2,1)} async-done(((bf16[32,8192]{1,0:T(8,128)(2,1)}), bf16[1024,8192]{1,0:T(8,128)(2,1)}) %all-gather.3.cloned.1.call-update) | async-done | bytes 16777232 | tf_op jit(solution)/shard_map/all_gather | solution.py:298
  157.5 25.0 %shard_map.132 = (bf16[256,1024]{1,0:T(8,128)(2,1)}, f32[256,768]{1,0:T(8,128)}) custom-call(bf16[256,1024]{1,0:T(8,128)(2,1)} %get-tuple-element.10.refs_0_, bf16[256,1024]{1,0:T(8,128)(2,1)} %refs_1_.3, f32[256,1024]{1,0:T(8,128)} %get-tuple-element.11.refs_2_, bf16[1024,8192]{1,0:T(8,128)(2,1)} %all-gather.3.cloned.1.call-done.refs_3_, ...), custom_call_target="tpu_custom_call" | custom-call | tf_op jit(solution)/shard_map/pallas_call | solution.py:346
  (3 shorter events, 0.1 us)
Async XLA Ops:
  7.2 150.3 %all-gather.3.cloned.1.call-start = ((), (), s32[]{:S(2)}) async-start(), calls=%async_computation.1 | async-start | bytes 17301504 | tf_op jit(solution)/shard_map/all_gather | solution.py:298
  46.4 69.7 %copy-start = (s32[1,256]{1,0:T(1,128)S(1)}, s32[1,256]{1,0:T(1,128)}, u32[]{:S(2)}) copy-start(s32[1,256]{1,0:T(1,128)} %refs_6_.1) | copy-start | bytes 3076
  105.3 17.8 %collective-permute-start = (bf16[512,4096]{1,0:T(8,128)(2,1)}, bf16[512,4096]{1,0:T(8,128)(2,1)}, u32[]{:S(2)}, u32[]{:S(2)}) collective-permute-start(bf16[512,4096]{1,0:T(8,128)(2,1)} %bitcast.7.refs_8_.refs_10_.refs_12_.refs_14_), channel_id=1, source_target_pairs={{0,16},{16,0},{32,48},{48,32},{64,80},{80,64},{96,112},{112,96},{1... | collective-permute-start | bytes 12582920 | tf_op jit(solution)/shard_map/ppermute | solution.py:305
Sparse Core Ops, SparseCore 0:
  44.6 112.8 all-gather.2

commit v4 on v3

v4 whole, which is shorter than its diff:
```python
import math

import jax
import jax.numpy as jnp
from jax import lax
from jax.experimental import pallas as pl
from jax.experimental.pallas import tpu as pltpu
from jax.sharding import PartitionSpec as P

HEADS = 16
STEP_SIZE = 0.1
VMEM_LIMIT = 56 * 1024 * 1024
F32 = jnp.float32
BF16 = jnp.bfloat16


def mm(a, b):
    return lax.dot_general(a, b, (((1,), (0,)), ((), ())), preferred_element_type=F32)


def mm_nt(a, b):
    return lax.dot_general(a, b, (((1,), (1,)), ((), ())), preferred_element_type=F32)


def mm_tn(a, b):
    return lax.dot_general(a, b, (((0,), (0,)), ((), ())), preferred_element_type=F32)


def normalize(values):
    center = jnp.mean(values, -1, keepdims=True)
    shifted = values - center
    spread = jnp.mean(shifted * shifted, -1, keepdims=True)
    inv = lax.rsqrt(spread + 1e-05)
    return shifted * inv, inv


def norm_back(values, gain, upstream):
    hat, inv = normalize(values)
    scaled = upstream * gain
    return inv * (
        scaled
        - jnp.mean(scaled, -1, keepdims=True)
        - hat * jnp.mean(scaled * hat, -1, keepdims=True)
    )


def head_mask(shape, head, size):
    lane = lax.broadcasted_iota(jnp.int32, shape, 1)
    return (lane >= head * size) & (lane < (head + 1) * size)


def softmax_shares(query, keys, same, scale):
    scores = mm_nt(query, keys) * scale
    powers = jnp.where(same, jnp.exp(scores), 0.0)
    return powers * (1.0 / jnp.sum(powers, -1, keepdims=True))


def embed_kernel(pix_ref, pert_ref, weight_ref, gain_ref, emb_ref, n1_ref):
    inputs = (pix_ref[...] + pert_ref[...]).astype(BF16)
    embedded = mm(inputs, weight_ref[...])
    emb_ref[...] = embedded
    n1_ref[...] = (normalize(embedded)[0] * gain_ref[...]).astype(BF16)


def columns(buf, first, last):
    sites, cores, chunk, width = buf.shape
    model = sites * cores * chunk
    return buf[:, :, :, first * model : last * model].reshape(model, (last - first) * model)


def attention_kernel(
    size,
    n1_hbm, emb_hbm, near_hbm, far_hbm, gain_ref, col_ref, row_ref,
    qkv_hbm, low_hbm, turned_hbm, mid_ref, n2_ref,
    n1_ref, emb_ref, attn_buf, qkv_buf, low_buf, turned_buf, att_ref, in_sem, low_sem, turned_sem, qkv_sem,
):
    rows, model = n1_ref.shape
    core = lax.rem(lax.axis_index("rows"), 2)
    pairs = (
        (n1_hbm, n1_ref),
        (near_hbm, attn_buf.at[:, core]),
        (far_hbm, attn_buf.at[:, 1 - core]),
        (emb_hbm, emb_ref),
    )
    copies = [pltpu.make_async_copy(*pair, in_sem.at[i]) for i, pair in enumerate(pairs)]
    for copy in copies:
        copy.start()
    for copy in copies:
        copy.wait()
    n1 = n1_ref[...]
    for which in range(3):
        qkv_buf[which] = mm(n1, columns(attn_buf, which, which + 1)).astype(BF16)
    qkv_copy = pltpu.make_async_copy(qkv_buf, qkv_hbm, qkv_sem)
    qkv_copy.start()
    quad = 4 * size
    scale = 1.0 / math.sqrt(size)
    same = col_ref[...] == row_ref[...]

    def low_copy(j):
        part = pl.ds(j * 4, 4)
        return pltpu.make_async_copy(low_buf.at[part], low_hbm.at[part], low_sem.at[j])

    def turned_copy(j):
        part = pl.ds(j * 4, 4)
        return pltpu.make_async_copy(turned_buf.at[part], turned_hbm.at[part], turned_sem.at[j])

    def step(j, carry):
        lanes = pl.ds(pl.multiple_of(j * quad, quad), quad)
        query, keys, vals = qkv_buf[0, :, lanes], qkv_buf[1, :, lanes], qkv_buf[2, :, lanes]
        zero = jnp.zeros_like(query)
        attended = jnp.zeros((rows, quad), F32)
        for head in range(4):
            mask = head_mask((rows, quad), head, size)
            shares = softmax_shares(jnp.where(mask, query, zero), keys, same, scale)
            low = shares.astype(BF16)
            low_buf[j * 4 + head] = low
            turned_buf[j * 4 + head] = shares.T.astype(BF16)
            attended = jnp.where(mask, mm(low, vals), attended)
        att_ref[:, lanes] = attended.astype(BF16)
        low_copy(j).start()
        turned_copy(j).start()
        return carry

    lax.fori_loop(0, model // quad, step, 0)
    mid = emb_ref[...] + mm_nt(att_ref[...], columns(attn_buf, 3, 4))
    mid_ref[...] = mid
    n2_ref[...] = (normalize(mid)[0] * gain_ref[...]).astype(BF16)
    qkv_copy.wait()
    for j in range(model // quad):
        low_copy(j).wait()
        turned_copy(j).wait()


def mlp_kernel(
    n2_hbm, og_hbm, weights_hbm, up_ref, out_ref,
    n2_ref, og_ref, up_buf, down_buf, acc_out, acc_grad, up_sem, down_sem, sem,
):
    chunks, _, width = up_buf.shape

    def up_copy(j):
        start = pl.multiple_of(j * width, width)
        source = weights_hbm.at[:, pl.ds(start, width)]
        return pltpu.make_async_copy(source, up_buf.at[j], up_sem.at[j])

    def down_copy(j):
        start = pl.multiple_of((chunks + j) * width, width)
        source = weights_hbm.at[:, pl.ds(start, width)]
        return pltpu.make_async_copy(source, down_buf.at[j], down_sem.at[j])

    first = pltpu.make_async_copy(n2_hbm, n2_ref, sem.at[0])
    second = pltpu.make_async_copy(og_hbm, og_ref, sem.at[1])
    first.start()
    up_copy(0).start()
    second.start()
    down_copy(0).start()
    for j in range(1, chunks):
        up_copy(j).start()
        down_copy(j).start()
    acc_out[...] = jnp.zeros_like(acc_out)
    acc_grad[...] = jnp.zeros_like(acc_grad)
    first.wait()
    second.wait()

    def step(j, carry):
        up_copy(j).wait()
        pre = mm(n2_ref[...], up_buf[j])
        down_copy(j).wait()
        grad_hidden = mm(og_ref[...], down_buf[j])
        root = math.sqrt(2.0 / math.pi)
        square = pre * pre
        tanh = jnp.tanh(root * pre * (1.0 + 0.044715 * square))
        half = 0.5 * (1.0 + tanh)
        act = (pre * half).astype(BF16)
        slope = half + 0.5 * pre * (1.0 - tanh * tanh) * (root * (1.0 + 3.0 * 0.044715 * square))
        grad_pre = (grad_hidden * slope).astype(BF16)
        acc_grad[...] += mm_nt(grad_pre, up_buf[j])
        acc_out[...] += mm_nt(act, down_buf[j])
        return carry

    lax.fori_loop(0, chunks, step, 0)
    up_ref[...] = acc_grad[...].astype(BF16)
    out_ref[...] = acc_out[...].astype(BF16)


def backward_kernel(
    size, images,
    og_hbm, mid_hbm, mine_hbm, theirs_hbm, near_out_hbm, far_out_hbm, qkv_hbm, low_hbm, turned_hbm,
    near_hbm, far_hbm, emb_hbm, emb_w_hbm, pert_hbm,
    gain1_ref, gain2_ref, ball_ref, col_ref,
    new_ref,
    og_ref, mid_ref, mine_ref, theirs_ref, attn_buf, qkv_buf, low_buf, turned_buf,
    emb_ref, emb_w_ref, pert_ref, acc_grad, heads_ref, proj_ref, sem,
):
    rows, model = og_ref.shape
    core = lax.rem(lax.axis_index("rows"), 2)
    head_part = pl.ds(0, 3 * model)
    out_part = pl.ds(3 * model, model)
    pairs = (
        (og_hbm, og_ref),
        (mid_hbm, mid_ref),
        (mine_hbm, mine_ref),
        (theirs_hbm, theirs_ref),
        (near_out_hbm.at[:, :, out_part], attn_buf.at[:, core, :, out_part]),
        (far_out_hbm.at[:, :, out_part], attn_buf.at[:, 1 - core, :, out_part]),
        (qkv_hbm, qkv_buf),
        (low_hbm, low_buf),
        (turned_hbm, turned_buf),
        (near_hbm.at[:, :, head_part], attn_buf.at[:, core, :, head_part]),
        (far_hbm.at[:, :, head_part], attn_buf.at[:, 1 - core, :, head_part]),
        (emb_hbm, emb_ref),
        (emb_w_hbm, emb_w_ref),
        (pert_hbm, pert_ref),
    )
    copies = [pltpu.make_async_copy(*pair, sem.at[i]) for i, pair in enumerate(pairs)]
    for copy in copies:
        copy.start()
    for copy in copies[:4]:
        copy.wait()
    grad_norm_two = mine_ref[...].astype(F32) + theirs_ref[...].astype(F32)
    grad_mid = og_ref[...].astype(F32) + norm_back(mid_ref[...], gain2_ref[...], grad_norm_two)
    acc_grad[...] = grad_mid
    for copy in copies[4:6]:
        copy.wait()
    heads_ref[...] = mm(grad_mid.astype(BF16), columns(attn_buf, 3, 4)).astype(BF16)
    for copy in copies[6:9]:
        copy.wait()
    quad = 4 * size
    scale = 1.0 / math.sqrt(size)

    def attention_step(j, carry):
        lanes = pl.ds(pl.multiple_of(j * quad, quad), quad)
        query, keys, vals = qkv_buf[0, :, lanes], qkv_buf[1, :, lanes], qkv_buf[2, :, lanes]
        grad_heads = heads_ref[:, lanes]
        zero = jnp.zeros_like(grad_heads)
        grad_query = jnp.zeros((rows, quad), F32)
        grad_keys = jnp.zeros((rows, quad), F32)
        grad_vals = jnp.zeros((rows, quad), F32)
        for head in range(4):
            mask = head_mask((rows, quad), head, size)
            shares = low_buf[j * 4 + head].astype(F32)
            grad_shares = mm_nt(jnp.where(mask, grad_heads, zero), vals)
            grad_vals = jnp.where(mask, mm(turned_buf[j * 4 + head], grad_heads), grad_vals)
            inner = jnp.sum(grad_shares * shares, -1, keepdims=True)
            grad_scores = (shares * (grad_shares - inner) * scale).astype(BF16)
            grad_query = jnp.where(mask, mm(grad_scores, keys), grad_query)
            grad_keys = jnp.where(mask, mm_tn(grad_scores, query), grad_keys)
        for which, value in enumerate((grad_query, grad_keys, grad_vals)):
            start = pl.multiple_of(which * model + j * quad, quad)
            proj_ref[:, pl.ds(start, quad)] = value.astype(BF16)
        return carry

    lax.fori_loop(0, model // quad, attention_step, 0)
    for copy in copies[9:]:
        copy.wait()
    grad_norm = mm_nt(proj_ref[...], columns(attn_buf, 0, 3))
    grad_embed = acc_grad[...] + norm_back(emb_ref[...], gain1_ref[...], grad_norm)
    grad_input = mm_nt(grad_embed.astype(BF16), emb_w_ref[...])
    labels = col_ref[...]
    noise = pert_ref[...]
    patch = noise.shape[1]
    row_sq = jnp.sum(grad_input * grad_input, -1, keepdims=True)
    scale_rows = jnp.zeros_like(row_sq)
    counts = []
    for image in range(images):
        own = labels == image
        count = jnp.sum(jnp.where(own, 1.0, 0.0), 0, keepdims=True) * patch
        counts.append(count)
        total = jnp.sum(jnp.where(own, row_sq, 0.0), 0, keepdims=True)
        scale_rows = jnp.where(own, STEP_SIZE * lax.rsqrt(total / count + 1e-06), scale_rows)
    candidate = noise + scale_rows * grad_input
    row_sq = jnp.sum(candidate * candidate, -1, keepdims=True)
    factor_rows = jnp.zeros_like(row_sq)
    for image in range(images):
        own = labels == image
        total = jnp.sum(jnp.where(own, row_sq, 0.0), 0, keepdims=True)
        factor = jnp.minimum(
            1.0, ball_ref[:, image : image + 1] * lax.rsqrt(total / counts[image] + 1e-06)
        )
        factor_rows = jnp.where(own, factor, factor_rows)
    new_ref[...] = candidate * factor_rows


def block(*shape, dtype=BF16):
    return pltpu.VMEM(shape, dtype)


def params():
    return pltpu.CompilerParams(vmem_limit_bytes=VMEM_LIMIT)


def body(
    pixels,
    perturbation,
    segment_ids,
    ball_radius,
    w_embed,
    gain_attn,
    w_qkv,
    w_out,
    gain_mlp,
    w_up,
    w_down,
    out_grad,
):
    rows, patch = pixels.shape
    model = w_embed.shape[1]
    chunk, _, share = w_qkv.shape
    units = w_up.shape[1]
    size = model // HEADS
    groups = model // share
    images = ball_radius.shape[1]

    mine = jnp.concatenate([w_qkv.reshape(chunk, 3 * share), w_out.T, w_up, w_down.T], 1)
    chunks = lax.all_gather(mine, "heads", axis=0, tiled=False)
    attn = chunks[:, :, : 4 * share].reshape(groups, chunk, 4, share)
    attn = attn.transpose(1, 2, 0, 3).reshape(chunk, 4 * model)
    half = lax.axis_index("heads") % 2
    mlp = chunks[:, :, 4 * share :].reshape(2, groups // 2, chunk, 2, units)
    mlp = lax.dynamic_index_in_dim(mlp, half, 0, keepdims=False)
    mlp = mlp.transpose(1, 2, 0, 3).reshape(chunk, groups * units)
    weights = lax.all_gather(mlp, "rows", axis=0, tiled=True)

    sites = lax.axis_size("rows") // 2
    planes = [[2 * site + core for site in range(sites)] for core in range(2)]
    copies = jnp.broadcast_to(attn[None], (sites,) + attn.shape)
    near = lax.all_to_all(copies, "rows", 0, 0, axis_index_groups=planes)
    near = near.reshape(sites * chunk, 4 * model)
    far = lax.ppermute(near, "rows", [(row, row ^ 1) for row in range(2 * sites)])

    shard = (sites, chunk, 4 * model)
    near, far = near.reshape(shard), far.reshape(shard)

    labels_col = segment_ids.reshape(rows, 1)
    labels_row = segment_ids.reshape(1, rows)
    gain1 = gain_attn.reshape(1, model)
    gain2 = gain_mlp.reshape(1, model)
    quads = model // (4 * size)
    full = lambda dt: jax.ShapeDtypeStruct((rows, model), dt)
    vmem = pl.BlockSpec(memory_space=pltpu.VMEM)
    outside = pl.BlockSpec(memory_space=pl.ANY)
    semaphores = pltpu.SemaphoreType.DMA

    embedded, normed_one = pl.pallas_call(
        embed_kernel,
        in_specs=[vmem] * 4,
        out_specs=[vmem] * 2,
        out_shape=[full(F32), full(BF16)],
        compiler_params=params(),
        cost_estimate=pl.CostEstimate(
            flops=2 * rows * patch * model, bytes_accessed=5 * 1024 * 1024, transcendentals=0
        ),
    )(pixels, perturbation, w_embed, gain1)

    squares = jax.ShapeDtypeStruct((HEADS, rows, rows), BF16)
    qkv, low, turned, stream_mid, normed_two = pl.pallas_call(
        lambda *refs: attention_kernel(size, *refs),
        in_specs=[outside] * 4 + [vmem] * 3,
        out_specs=[outside] * 3 + [vmem] * 2,
        out_shape=[jax.ShapeDtypeStruct((3, rows, model), BF16), squares, squares]
        + [full(F32), full(BF16)],
        scratch_shapes=[
            block(rows, model),
            block(rows, model, dtype=F32),
            block(sites, 2, chunk, 4 * model),
            block(3, rows, model),
            block(HEADS, rows, rows),
            block(HEADS, rows, rows),
            block(rows, model),
            semaphores((4,)),
            semaphores((quads,)),
            semaphores((quads,)),
            semaphores,
        ],
        compiler_params=params(),
    )(normed_one, embedded, near, far, gain2, labels_col, labels_row)

    width = 512
    count = groups * units // 2 // width
    up_mine, out_mine = pl.pallas_call(
        mlp_kernel,
        in_specs=[outside] * 3,
        out_specs=[vmem] * 2,
        out_shape=[full(BF16), full(BF16)],
        scratch_shapes=[
            block(rows, model),
            block(rows, model),
            block(count, model, width),
            block(count, model, width),
            block(rows, model, dtype=F32),
            block(rows, model, dtype=F32),
            semaphores((count,)),
            semaphores((count,)),
            semaphores((2,)),
        ],
        compiler_params=params(),
    )(normed_two, out_grad, weights)

    pairs = [(group, group ^ 1) for group in range(groups)]
    up_theirs = lax.ppermute(up_mine, "heads", pairs)
    out_mine, up_theirs = lax.optimization_barrier((out_mine, up_theirs))
    out_theirs = lax.ppermute(out_mine, "heads", pairs)

    moved = (out_grad, stream_mid, up_mine, up_theirs, near, far, qkv, low, turned)
    moved = moved + (near, far, embedded, w_embed, perturbation)
    updated = pl.pallas_call(
        lambda *refs: backward_kernel(size, images, *refs),
        in_specs=[outside] * len(moved) + [vmem] * 4,
        out_specs=vmem,
        out_shape=jax.ShapeDtypeStruct((rows, patch), F32),
        scratch_shapes=[
            block(rows, model),
            block(rows, model, dtype=F32),
            block(rows, model),
            block(rows, model),
            block(sites, 2, chunk, 4 * model),
            block(3, rows, model),
            block(HEADS, rows, rows),
            block(HEADS, rows, rows),
            block(rows, model, dtype=F32),
            block(patch, model),
            block(rows, patch, dtype=F32),
            block(rows, model, dtype=F32),
            block(rows, model),
            block(rows, 3 * model),
            semaphores((len(moved),)),
        ],
        compiler_params=params(),
        cost_estimate=pl.CostEstimate(
            flops=16 * rows * model * model, bytes_accessed=20 * 1024 * 1024, transcendentals=0
        ),
    )(*moved, gain1, gain2, ball_radius, labels_col)
    block_out = stream_mid + (out_mine.astype(F32) + out_theirs.astype(F32))
    return (block_out.astype(BF16), updated)


def solution(mesh):
    in_specs = (
        P("rows", None),
        P("rows", None),
        P("rows", None),
        P("rows", None),
        P(),
        P(),
        P("rows", None, "heads"),
        P("heads", "rows"),
        P(),
        P("rows", "heads"),
        P("heads", "rows"),
        P("rows", None),
    )
    out_specs = (P("rows", None), P("rows", None))
    return jax.shard_map(body, mesh=mesh, in_specs=in_specs, out_specs=out_specs, check_vma=False)
```

time: 190 us -> 189 us (level)
  starting transfers between devices: 10.8 us -> 17.2 us
  waiting for transfers between devices: 22.1 us -> 17.8 us
  blocking collectives: 92.8 us -> 88.9 us
  Pallas kernels: 41.3 us -> 43.3 us
    all_gather x1, waiting for transfers between devices: 18.1 us -> 2.96 us  [body(): weights = lax.all_gather(mlp, 'rows', axis=0, tiled=True)]
    ppermute x0 -> x2, waiting for transfers between devices: none -> 12.2 us  [the longest x1 12.2 us: body(): up_theirs = lax.ppermute(up_mine, 'heads', pairs)]
    ppermute x0 -> x2, starting transfers between devices: none -> 6.53 us  [the longest x1 3.35 us: body(): out_theirs = lax.ppermute(out_mine, 'heads', pairs)]
    all_to_all x1, blocking collectives: 58.9 us -> 55 us  [body(): near = lax.all_to_all(copies, 'rows', 0, 0, axis_index_groups=planes)]
    pallas_call x2 -> x4, Pallas kernels: 41.3 us -> 43.3 us  [the longest x1 15.4 us: body(): pl.pallas_call(lambda *refs: backward_kernel(size, images, *refs), in_spe...]
  transfers between devices with their start and end apart: 2 -> 4, of which waited for: 2 -> 3; matrix products, arithmetic and copies ran while one was open for 3% -> 1% of each run, Pallas kernels for 9% -> 17%
where the time goes in v4:
time: 189 us; the launch traced here: 188 us
  blocking collectives  88.9 us (47%)
  Pallas kernels  43.3 us (23%)
  waiting for transfers between devices  17.8 us (9%)
  starting transfers between devices  17.2 us (9%)
  between operations  14.2 us (8%)
  local copies, waits for them, and re-layouts  4.88 us (3%)
    all_to_all x1, blocking collectives, body(): near = lax.all_to_all(copies, 'rows', 0, 0, axis_index_groups=planes)  55 us
    all_gather x1, blocking collectives, body(): chunks = lax.all_gather(mine, 'heads', axis=0, tiled=False)  33.9 us
    pallas_call x1, Pallas kernels, body(): pl.pallas_call(lambda *refs: backward_kernel(size, images, *refs), in_spe...  15.4 us
    pallas_call x1, Pallas kernels, body(): pl.pallas_call(lambda *refs: attention_kernel(size, *refs), in_specs=[out...  12.9 us
    ppermute x1, waiting for transfers between devices, body(): up_theirs = lax.ppermute(up_mine, 'heads', pairs)  12.2 us
    pallas_call x1, Pallas kernels, body(): pl.pallas_call(mlp_kernel, in_specs=[outside] * 3, out_specs=[vmem] * 2,...  11 us
    ppermute x1, starting transfers between devices, body(): lax.ppermute(near, 'rows', [(row, row ^ 1) for row in range(2 * sites)])  10.7 us
    pallas_call x1, Pallas kernels, body(): pl.pallas_call(embed_kernel, in_specs=[vmem] * 4, out_specs=[vmem] * 2, o...  4.04 us
  transfers between devices with their start and end apart: 4, of which 3 were waited for; matrix products, arithmetic and copies ran while one was open for 1% of the time, Pallas kernels for 17%

profile of v4, /device:TPU:1, one launch (start us, length us, event | category | flops | bytes accessed | tf_op | source)
XLA Modules:
  0.0 188.1 jit_solution(7633882471227121614)
XLA Ops:
  7.2 0.8 copy.17
  8.1 0.8 pad_maximum_fusion
  8.9 33.9 %all-gather = bf16[512,768]{1,0:T(8,128)(2,1)S(1)} all-gather(bf16[32,768]{1,0:T(8,128)(2,1)S(1)} %pad_maximum_fusion), channel_id=2, replica_groups=mesh['rows'=32,'heads'=16] {'heads'}, dimensions={0}, use_global_device_ids=true | all-gather | bytes 835584 | tf_op jit(solution)/shard_map/all_gather | solution.py:314
  42.8 0.1 reshape.39
  43.0 0.2 constant_dynamic-slice_fusion
  43.2 0.2 copy.22
  43.4 0.8 copy.23
  44.2 0.2 reshape.34
  44.5 0.6 copy.25
  45.1 0.5 broadcast_in_dim.7
  45.6 0.5 broadcast_in_dim.8
  46.1 55.0 %all_to_all.5.refs_2_.refs_4_.refs_9_ = bf16[16,32,4096]{2,1,0:T(8,128)(2,1)} all-to-all(bf16[16,32,4096]{2,1,0:T(8,128)(2,1)S(1)} %broadcast_in_dim.8), channel_id=1, replica_groups={{0,32,64,96,128,160,192,224,256,288,320,352,384,416,448,480},{16,48,80,..., dimensions={0} | all-to-all | bytes 8388608 | tf_op jit(solution)/shard_map/all_to_all | solution.py:326
  101.1 10.7 %collective-permute-start = (bf16[512,4096]{1,0:T(8,128)(2,1)}, bf16[512,4096]{1,0:T(8,128)(2,1)}, u32[]{:S(2)}, u32[]{:S(2)}) collective-permute-start(bf16[512,4096]{1,0:T(8,128)(2,1)} %bitcast.5), channel_id=1, source_target_pairs={{0,16},{16,0},{32,48},{48,32},{64,80},{80,64},{96,112},{112,96},{1... | collective-permute-start | bytes 12582920 | tf_op jit(solution)/shard_map/ppermute | solution.py:328
  111.7 0.8 copy.19.refs_5_.refs_17_
  112.5 4.0 %shard_map.131 = (f32[256,1024]{1,0:T(8,128)}, bf16[256,1024]{1,0:T(8,128)(2,1)}) custom-call(f32[256,768]{1,0:T(8,128)} %pix_ref.1, f32[256,768]{1,0:T(8,128)} %refs_13_.1, bf16[768,1024]{1,0:T(8,128)(2,1)} %refs_12_.1, f32[1,1024]{1,0:T(1,128)} %bitcast.26), custom_call_target="tpu_custom_call" | custom-call | flops 402653184 | bytes 5242880 | tf_op jit(solution)/shard_map/pallas_call | solution.py:343
  116.6 2.6 %collective-permute-done = bf16[512,4096]{1,0:T(8,128)(2,1)} collective-permute-done((bf16[512,4096]{1,0:T(8,128)(2,1)}, bf16[512,4096]{1,0:T(8,128)(2,1)}, u32[]{:S(2)}, u32[]{:S(2)}) %collective-permute-start) | collective-permute-done | bytes 4194336 | tf_op jit(solution)/shard_map/ppermute | solution.py:328
  119.2 12.9 %shard_map.132 = (bf16[3,256,1024]{2,1,0:T(8,128)(2,1)}, bf16[16,256,256]{2,1,0:T(8,128)(2,1)}, bf16[16,256,256]{2,1,0:T(8,128)(2,1)}, f32[256,1024]{1,0:T(8,128)}, bf16[256,1024]{1,0:T(8,128)(2,1)}) custom-call(bf16[256,1024]{1,0:T(8,128)(2,1)} %get-tuple-element.13.refs_0_, f32[256,1024]{1,0:T(8,128)} %get-tuple-element.14.refs_1_.refs_11_, ...), custom_call_target="tpu_custom_call" | custom-call | tf_op jit(solution)/shard_map/pallas_call | solution.py:355
  132.1 3.0 %all-gather.3.cloned.1.call-done.weights_hbm = bf16[1024,4096]{1,0:T(8,128)(2,1)} async-done(((bf16[32,4096]{1,0:T(8,128)(2,1)}), bf16[1024,4096]{1,0:T(8,128)(2,1)}) %all-gather.3.cloned.1.call-update) | async-done | bytes 8388624 | tf_op jit(solution)/shard_map/all_gather | solution.py:321
  135.1 11.0 %shard_map.133 = (bf16[256,1024]{1,0:T(8,128)(2,1)}, bf16[256,1024]{1,0:T(8,128)(2,1)}) custom-call(bf16[256,1024]{1,0:T(8,128)(2,1)} %get-tuple-element.16.n2_hbm, bf16[256,1024]{1,0:T(8,128)(2,1)} %refs_0_.1, bf16[1024,4096]{1,0:T(8,128)(2,1)} %all-gather.3.cloned.1.call-done.weights_hbm), custom_call_target="tpu_custom_call" | custom-call | tf_op jit(solution)/shard_map/pallas_call | solution.py:379
  146.1 3.2 %collective-permute-start.1 = (bf16[256,1024]{1,0:T(8,128)(2,1)}, bf16[256,1024]{1,0:T(8,128)(2,1)S(1)}, u32[]{:S(2)}, u32[]{:S(2)}) collective-permute-start(bf16[256,1024]{1,0:T(8,128)(2,1)} %get-tuple-element.18.refs_2_), channel_id=1, source_target_pairs={{0,1},{1,0},{2,3},{3,2},{4,5},{5,4},{6,7},{7,6},{8,9},{9,8},{10,11... | collective-permute-start | bytes 1572872 | tf_op jit(solution)/shard_map/ppermute | solution.py:399
  149.2 12.2 %collective-permute-done.1.refs_3_ = bf16[256,1024]{1,0:T(8,128)(2,1)S(1)} collective-permute-done((bf16[256,1024]{1,0:T(8,128)(2,1)}, bf16[256,1024]{1,0:T(8,128)(2,1)S(1)}, u32[]{:S(2)}, u32[]{:S(2)}) %collective-permute-start.1) | collective-permute-done | bytes 524320 | tf_op jit(solution)/shard_map/ppermute | solution.py:399
  161.4 3.3 %collective-permute-start.2 = (bf16[256,1024]{1,0:T(8,128)(2,1)}, bf16[256,1024]{1,0:T(8,128)(2,1)S(1)}, u32[]{:S(2)}, u32[]{:S(2)}) collective-permute-start(bf16[256,1024]{1,0:T(8,128)(2,1)} %get-tuple-element.19), channel_id=1, source_target_pairs={{0,1},{1,0},{2,3},{3,2},{4,5},{5,4},{6,7},{7,6},{8,9},{9,8},{10,11... | collective-permute-start | bytes 1572872 | tf_op jit(solution)/shard_map/ppermute | solution.py:401
  164.8 15.4 %shard_map.134 = f32[256,768]{1,0:T(8,128)} custom-call(bf16[256,1024]{1,0:T(8,128)(2,1)} %refs_0_.1, f32[256,1024]{1,0:T(8,128)} %get-tuple-element.15.refs_1_, bf16[256,1024]{1,0:T(8,128)(2,1)} %get-tuple-element.18.refs_2_, bf16[256,1024]{1,0:T(8,128)(2,1)} %copy-done.1, bf16[16,32,4096]{2,1,0:T(8,128)(2,1)} %all_to_all.5.refs_2_.refs_4_.refs_9_, ...), custom_call_target="tpu_custom_call" | custom-call | flops 4294967296 | bytes 20971520 | tf_op jit(solution)/shard_map/pallas_call | solution.py:405
  180.2 1.0 add_convert_fusion
  (14 shorter events, 0.2 us)
Async XLA Ops:
  7.2 127.9 %all-gather.3.cloned.1.call-start = ((), (), s32[]{:S(2)}) async-start(), calls=%async_computation.1 | async-start | bytes 8650752 | tf_op jit(solution)/shard_map/all_gather | solution.py:321
  46.1 65.6 %copy-start.3 = (s32[1,256]{1,0:T(1,128)S(1)}, s32[1,256]{1,0:T(1,128)}, u32[]{:S(2)}) copy-start(s32[1,256]{1,0:T(1,128)} %refs_6_.1) | copy-start | bytes 3076
  101.1 18.1 %collective-permute-start = (bf16[512,4096]{1,0:T(8,128)(2,1)}, bf16[512,4096]{1,0:T(8,128)(2,1)}, u32[]{:S(2)}, u32[]{:S(2)}) collective-permute-start(bf16[512,4096]{1,0:T(8,128)(2,1)} %bitcast.5), channel_id=1, source_target_pairs={{0,16},{16,0},{32,48},{48,32},{64,80},{80,64},{96,112},{112,96},{1... | collective-permute-start | bytes 12582920 | tf_op jit(solution)/shard_map/ppermute | solution.py:328
  146.1 15.4 %collective-permute-start.1 = (bf16[256,1024]{1,0:T(8,128)(2,1)}, bf16[256,1024]{1,0:T(8,128)(2,1)S(1)}, u32[]{:S(2)}, u32[]{:S(2)}) collective-permute-start(bf16[256,1024]{1,0:T(8,128)(2,1)} %get-tuple-element.18.refs_2_), channel_id=1, source_target_pairs={{0,1},{1,0},{2,3},{3,2},{4,5},{5,4},{6,7},{7,6},{8,9},{9,8},{10,11... | collective-permute-start | bytes 1572872 | tf_op jit(solution)/shard_map/ppermute | solution.py:399
  161.4 3.4 %copy-start.1 = (bf16[256,1024]{1,0:T(8,128)(2,1)}, bf16[256,1024]{1,0:T(8,128)(2,1)S(1)}, u32[]{:S(2)}) copy-start(bf16[256,1024]{1,0:T(8,128)(2,1)S(1)} %collective-permute-done.1.refs_3_) | copy-start | bytes 1572868
  161.4 18.8 %collective-permute-start.2 = (bf16[256,1024]{1,0:T(8,128)(2,1)}, bf16[256,1024]{1,0:T(8,128)(2,1)S(1)}, u32[]{:S(2)}, u32[]{:S(2)}) collective-permute-start(bf16[256,1024]{1,0:T(8,128)(2,1)} %get-tuple-element.19), channel_id=1, source_target_pairs={{0,1},{1,0},{2,3},{3,2},{4,5},{5,4},{6,7},{7,6},{8,9},{9,8},{10,11... | collective-permute-start | bytes 1572872 | tf_op jit(solution)/shard_map/ppermute | solution.py:401
  164.8 15.4 %copy-start = (f32[256,1024]{1,0:T(8,128)S(1)}, f32[256,1024]{1,0:T(8,128)}, u32[]{:S(2)}) copy-start(f32[256,1024]{1,0:T(8,128)} %get-tuple-element.15.refs_1_) | copy-start | bytes 3145732
  164.8 15.4 %copy-start.2 = (bf16[256,1024]{1,0:T(8,128)(2,1)S(1)}, bf16[256,1024]{1,0:T(8,128)(2,1)}, u32[]{:S(2)}) copy-start(bf16[256,1024]{1,0:T(8,128)(2,1)} %get-tuple-element.19) | copy-start | bytes 1572868
Sparse Core Ops, SparseCore 0:
  44.3 90.6 all-gather.2

commit v5 on v4

--- a/solution.py
+++ b/solution.py
@@ -9,7 +9,7 @@
 
 HEADS = 16
 STEP_SIZE = 0.1
-VMEM_LIMIT = 56 * 1024 * 1024
+MIB = 1024 * 1024
 F32 = jnp.float32
 BF16 = jnp.bfloat16
 
@@ -76,19 +76,20 @@
 ):
     rows, model = n1_ref.shape
     core = lax.rem(lax.axis_index("rows"), 2)
-    pairs = (
-        (n1_hbm, n1_ref),
-        (near_hbm, attn_buf.at[:, core]),
-        (far_hbm, attn_buf.at[:, 1 - core]),
-        (emb_hbm, emb_ref),
-    )
+    pairs = [(n1_hbm, n1_ref)]
+    for which in range(4):
+        part = pl.ds(which * model, model)
+        pairs.append((near_hbm.at[:, :, part], attn_buf.at[:, core, :, part]))
+        pairs.append((far_hbm.at[:, :, part], attn_buf.at[:, 1 - core, :, part]))
+    pairs.append((emb_hbm, emb_ref))
     copies = [pltpu.make_async_copy(*pair, in_sem.at[i]) for i, pair in enumerate(pairs)]
     for copy in copies:
         copy.start()
-    for copy in copies:
-        copy.wait()
+    copies[0].wait()
     n1 = n1_ref[...]
     for which in range(3):
+        copies[1 + 2 * which].wait()
+        copies[2 + 2 * which].wait()
         qkv_buf[which] = mm(n1, columns(attn_buf, which, which + 1)).astype(BF16)
     qkv_copy = pltpu.make_async_copy(qkv_buf, qkv_hbm, qkv_sem)
     qkv_copy.start()
@@ -122,6 +123,8 @@
         return carry
 
     lax.fori_loop(0, model // quad, step, 0)
+    for copy in copies[7:]:
+        copy.wait()
     mid = emb_ref[...] + mm_nt(att_ref[...], columns(attn_buf, 3, 4))
     mid_ref[...] = mid
     n2_ref[...] = (normalize(mid)[0] * gain_ref[...]).astype(BF16)
@@ -161,11 +164,13 @@
     first.wait()
     second.wait()
 
-    def step(j, carry):
+    def front(j):
         up_copy(j).wait()
         pre = mm(n2_ref[...], up_buf[j])
         down_copy(j).wait()
-        grad_hidden = mm(og_ref[...], down_buf[j])
+        return pre, mm(og_ref[...], down_buf[j])
+
+    def back(j, pre, grad_hidden):
         root = math.sqrt(2.0 / math.pi)
         square = pre * pre
         tanh = jnp.tanh(root * pre * (1.0 + 0.044715 * square))
@@ -175,55 +180,43 @@
         grad_pre = (grad_hidden * slope).astype(BF16)
         acc_grad[...] += mm_nt(grad_pre, up_buf[j])
         acc_out[...] += mm_nt(act, down_buf[j])
-        return carry
-
-    lax.fori_loop(0, chunks, step, 0)
+
+    now = front(0)
+    for j in range(chunks):
+        later = front(j + 1) if j + 1 < chunks else None
+        back(j, *now)
+        now = later
     up_ref[...] = acc_grad[...].astype(BF16)
     out_ref[...] = acc_out[...].astype(BF16)
 
 
 def backward_kernel(
     size, images,
-    og_hbm, mid_hbm, mine_hbm, theirs_hbm, near_out_hbm, far_out_hbm, qkv_hbm, low_hbm, turned_hbm,
-    near_hbm, far_hbm, emb_hbm, emb_w_hbm, pert_hbm,
-    gain1_ref, gain2_ref, ball_ref, col_ref,
+    near_hbm, far_hbm,
+    og_ref, mid_ref, mine_ref, theirs_ref, qkv_buf, low_buf, turned_buf,
+    emb_ref, emb_w_ref, pert_ref, gain1_ref, gain2_ref, ball_ref, col_ref,
     new_ref,
-    og_ref, mid_ref, mine_ref, theirs_ref, attn_buf, qkv_buf, low_buf, turned_buf,
-    emb_ref, emb_w_ref, pert_ref, acc_grad, heads_ref, proj_ref, sem,
+    attn_buf, acc_grad, heads_ref, proj_ref, sem,
 ):
     rows, model = og_ref.shape
     core = lax.rem(lax.axis_index("rows"), 2)
     head_part = pl.ds(0, 3 * model)
     out_part = pl.ds(3 * model, model)
     pairs = (
-        (og_hbm, og_ref),
-        (mid_hbm, mid_ref),
-        (mine_hbm, mine_ref),
-        (theirs_hbm, theirs_ref),
-        (near_out_hbm.at[:, :, out_part], attn_buf.at[:, core, :, out_part]),
-        (far_out_hbm.at[:, :, out_part], attn_buf.at[:, 1 - core, :, out_part]),
-        (qkv_hbm, qkv_buf),
-        (low_hbm, low_buf),
-        (turned_hbm, turned_buf),
+        (near_hbm.at[:, :, out_part], attn_buf.at[:, core, :, out_part]),
+        (far_hbm.at[:, :, out_part], attn_buf.at[:, 1 - core, :, out_part]),
         (near_hbm.at[:, :, head_part], attn_buf.at[:, core, :, head_part]),
         (far_hbm.at[:, :, head_part], attn_buf.at[:, 1 - core, :, head_part]),
-        (emb_hbm, emb_ref),
-        (emb_w_hbm, emb_w_ref),
-        (pert_hbm, pert_ref),
     )
     copies = [pltpu.make_async_copy(*pair, sem.at[i]) for i, pair in enumerate(pairs)]
     for copy in copies:
         copy.start()
-    for copy in copies[:4]:
-        copy.wait()
     grad_norm_two = mine_ref[...].astype(F32) + theirs_ref[...].astype(F32)
     grad_mid = og_ref[...].astype(F32) + norm_back(mid_ref[...], gain2_ref[...], grad_norm_two)
     acc_grad[...] = grad_mid
-    for copy in copies[4:6]:
+    for copy in copies[:2]:
         copy.wait()
     heads_ref[...] = mm(grad_mid.astype(BF16), columns(attn_buf, 3, 4)).astype(BF16)
-    for copy in copies[6:9]:
-        copy.wait()
     quad = 4 * size
     scale = 1.0 / math.sqrt(size)
 
@@ -250,7 +243,7 @@
         return carry
 
     lax.fori_loop(0, model // quad, attention_step, 0)
-    for copy in copies[9:]:
+    for copy in copies[2:]:
         copy.wait()
     grad_norm = mm_nt(proj_ref[...], columns(attn_buf, 0, 3))
     grad_embed = acc_grad[...] + norm_back(emb_ref[...], gain1_ref[...], grad_norm)
@@ -284,8 +277,8 @@
     return pltpu.VMEM(shape, dtype)
 
 
-def params():
-    return pltpu.CompilerParams(vmem_limit_bytes=VMEM_LIMIT)
+def params(mib):
+    return pltpu.CompilerParams(vmem_limit_bytes=mib * MIB)
 
 
 def body(
@@ -345,7 +338,7 @@
         in_specs=[vmem] * 4,
         out_specs=[vmem] * 2,
         out_shape=[full(F32), full(BF16)],
-        compiler_params=params(),
+        compiler_params=params(12),
         cost_estimate=pl.CostEstimate(
             flops=2 * rows * patch * model, bytes_accessed=5 * 1024 * 1024, transcendentals=0
         ),
@@ -366,15 +359,15 @@
             block(HEADS, rows, rows),
             block(HEADS, rows, rows),
             block(rows, model),
-            semaphores((4,)),
+            semaphores((10,)),
             semaphores((quads,)),
             semaphores((quads,)),
             semaphores,
         ],
-        compiler_params=params(),
+        compiler_params=params(56),
     )(normed_one, embedded, near, far, gain2, labels_col, labels_row)
 
-    width = 512
+    width = 1024
     count = groups * units // 2 // width
     up_mine, out_mine = pl.pallas_call(
         mlp_kernel,
@@ -392,43 +385,33 @@
             semaphores((count,)),
             semaphores((2,)),
         ],
-        compiler_params=params(),
+        compiler_params=params(49),
     )(normed_two, out_grad, weights)
 
     pairs = [(group, group ^ 1) for group in range(groups)]
     up_theirs = lax.ppermute(up_mine, "heads", pairs)
-    out_mine, up_theirs = lax.optimization_barrier((out_mine, up_theirs))
     out_theirs = lax.ppermute(out_mine, "heads", pairs)
 
-    moved = (out_grad, stream_mid, up_mine, up_theirs, near, far, qkv, low, turned)
-    moved = moved + (near, far, embedded, w_embed, perturbation)
+    held = (out_grad, stream_mid, up_mine, up_theirs, qkv, low, turned, embedded, w_embed)
+    held = held + (perturbation, gain1, gain2, ball_radius, labels_col)
     updated = pl.pallas_call(
         lambda *refs: backward_kernel(size, images, *refs),
-        in_specs=[outside] * len(moved) + [vmem] * 4,
+        in_specs=[outside] * 2 + [vmem] * len(held),
         out_specs=vmem,
         out_shape=jax.ShapeDtypeStruct((rows, patch), F32),
         scratch_shapes=[
-            block(rows, model),
-            block(rows, model, dtype=F32),
-            block(rows, model),
-            block(rows, model),
             block(sites, 2, chunk, 4 * model),
-            block(3, rows, model),
-            block(HEADS, rows, rows),
-            block(HEADS, rows, rows),
-            block(rows, model, dtype=F32),
-            block(patch, model),
-            block(rows, patch, dtype=F32),
             block(rows, model, dtype=F32),
             block(rows, model),
             block(rows, 3 * model),
-            semaphores((len(moved),)),
+            semaphores((4,)),
         ],
-        compiler_params=params(),
+        compiler_params=params(30),
         cost_estimate=pl.CostEstimate(
             flops=16 * rows * model * model, bytes_accessed=20 * 1024 * 1024, transcendentals=0
         ),
-    )(*moved, gain1, gain2, ball_radius, labels_col)
+    )(near, far, *held)
+    out_theirs, updated = lax.optimization_barrier((out_theirs, updated))
     block_out = stream_mid + (out_mine.astype(F32) + out_theirs.astype(F32))
     return (block_out.astype(BF16), updated)
 

time: 189 us -> 180 us (0.952)
  Pallas kernels: 43.3 us -> 31.5 us
  local copies, waits for them, and re-layouts: 4.88 us -> 7.77 us
    pallas_call x1, Pallas kernels: 11 us -> 7.21 us  [body(): pl.pallas_call(mlp_kernel, in_specs=[outside] * 3, out_specs=[vmem] * 2,...]
    pallas_call x1, Pallas kernels: 4.04 us -> 0.84 us  [body(): pl.pallas_call(embed_kernel, in_specs=[vmem] * 4, out_specs=[vmem] * 2, o...]
    pallas_call x1, Pallas kernels: 15.4 us -> 12.4 us  [body(): pl.pallas_call(lambda *refs: backward_kernel(size, images, *refs), in_spe...]
    unnamed x11 -> x37, local copies, waits for them, and re-layouts: 1.81 us -> 4.69 us
    ppermute x1, waiting for transfers between devices: 12.2 us -> 9.68 us  [body(): up_theirs = lax.ppermute(up_mine, 'heads', pairs)]
  transfers between devices with their start and end apart: 4 -> 4, of which waited for: 3 -> 3; matrix products, arithmetic and copies ran while one was open for 1% -> 1% of each run, Pallas kernels for 17% -> 14%
where the time goes in v5:
time: 180 us; the launch traced here: 179 us
  blocking collectives  89.1 us (50%)
  Pallas kernels  31.5 us (18%)
  waiting for transfers between devices  18.5 us (10%)
  starting transfers between devices  16.2 us (9%)
  between operations  14.3 us (8%)
  local copies, waits for them, and re-layouts  7.77 us (4%)
  other arithmetic  1.85 us (1%)
    all_to_all x1, blocking collectives, body(): near = lax.all_to_all(copies, 'rows', 0, 0, axis_index_groups=planes)  55.2 us
    all_gather x1, blocking collectives, body(): chunks = lax.all_gather(mine, 'heads', axis=0, tiled=False)  33.9 us
    pallas_call x1, Pallas kernels, body(): pl.pallas_call(lambda *refs: backward_kernel(size, images, *refs), in_spe...  12.4 us
    pallas_call x1, Pallas kernels, body(): pl.pallas_call(lambda *refs: attention_kernel(size, *refs), in_specs=[out...  11.1 us
    ppermute x1, starting transfers between devices, body(): lax.ppermute(near, 'rows', [(row, row ^ 1) for row in range(2 * sites)])  10.7 us
    ppermute x1, waiting for transfers between devices, body(): up_theirs = lax.ppermute(up_mine, 'heads', pairs)  9.68 us
    pallas_call x1, Pallas kernels, body(): pl.pallas_call(mlp_kernel, in_specs=[outside] * 3, out_specs=[vmem] * 2,...  7.21 us
    all_gather x1, waiting for transfers between devices, body(): weights = lax.all_gather(mlp, 'rows', axis=0, tiled=True)  4.82 us
  transfers between devices with their start and end apart: 4, of which 3 were waited for; matrix products, arithmetic and copies ran while one was open for 1% of the time, Pallas kernels for 14%

profile of v5, /device:TPU:1, one launch (start us, length us, event | category | flops | bytes accessed | tf_op | source)
XLA Modules:
  0.0 179.2 jit_solution(10937710502285920712)
XLA Ops:
  7.2 0.8 copy.17
  8.1 0.8 pad_maximum_fusion
  8.9 33.9 %all-gather = bf16[512,768]{1,0:T(8,128)(2,1)S(1)} all-gather(bf16[32,768]{1,0:T(8,128)(2,1)S(1)} %pad_maximum_fusion), channel_id=2, replica_groups=mesh['rows'=32,'heads'=16] {'heads'}, dimensions={0}, use_global_device_ids=true | all-gather | bytes 835584 | tf_op jit(solution)/shard_map/all_gather | solution.py:307
  43.4 0.8 copy.23
  44.3 0.2 reshape.34
  44.5 0.6 copy.25
  45.1 0.5 broadcast_in_dim.7
  45.6 0.5 broadcast_in_dim.8
  46.2 55.2 %all_to_all.5.refs_2_.refs_0_ = bf16[16,32,4096]{2,1,0:T(8,128)(2,1)} all-to-all(bf16[16,32,4096]{2,1,0:T(8,128)(2,1)S(1)} %broadcast_in_dim.8), channel_id=1, replica_groups={{0,32,64,96,128,160,192,224,256,288,320,352,384,416,448,480},{16,48,80,..., dimensions={0} | all-to-all | bytes 8388608 | tf_op jit(solution)/shard_map/all_to_all | solution.py:319
  101.4 10.7 %collective-permute-start = (bf16[512,4096]{1,0:T(8,128)(2,1)}, bf16[512,4096]{1,0:T(8,128)(2,1)}, u32[]{:S(2)}, u32[]{:S(2)}) collective-permute-start(bf16[512,4096]{1,0:T(8,128)(2,1)} %bitcast.5), channel_id=1, source_target_pairs={{0,16},{16,0},{32,48},{48,32},{64,80},{80,64},{96,112},{112,96},{1... | collective-permute-start | bytes 12582920 | tf_op jit(solution)/shard_map/ppermute | solution.py:321
  112.1 0.8 copy.19.refs_5_.refs_15_
  112.9 0.8 shard_map.131
  113.7 1.0 copy-done.1
  114.7 0.8 copy-done.12
  115.5 4.0 %collective-permute-done = bf16[512,4096]{1,0:T(8,128)(2,1)} collective-permute-done((bf16[512,4096]{1,0:T(8,128)(2,1)}, bf16[512,4096]{1,0:T(8,128)(2,1)}, u32[]{:S(2)}, u32[]{:S(2)}) %collective-permute-start) | collective-permute-done | bytes 4194336 | tf_op jit(solution)/shard_map/ppermute | solution.py:321
  119.5 11.1 %shard_map.132 = (bf16[3,256,1024]{2,1,0:T(8,128)(2,1)}, bf16[16,256,256]{2,1,0:T(8,128)(2,1)}, bf16[16,256,256]{2,1,0:T(8,128)(2,1)}, f32[256,1024]{1,0:T(8,128)}, bf16[256,1024]{1,0:T(8,128)(2,1)}) custom-call(bf16[256,1024]{1,0:T(8,128)(2,1)} %copy-done.12, f32[256,1024]{1,0:T(8,128)} %copy-done.1, bf16[16,32,4096]{2,1,0:T(8,128)(2,1)} %all_to_all.5.refs_2_.refs_0_, ...), custom_call_target="tpu_custom_call" | custom-call | tf_op jit(solution)/shard_map/pallas_call | solution.py:348
  130.6 4.8 %all-gather.3.cloned.1.call-done.weights_hbm = bf16[1024,4096]{1,0:T(8,128)(2,1)} async-done(((bf16[32,4096]{1,0:T(8,128)(2,1)}), bf16[1024,4096]{1,0:T(8,128)(2,1)}) %all-gather.3.cloned.1.call-update) | async-done | bytes 8388624 | tf_op jit(solution)/shard_map/all_gather | solution.py:314
  135.4 1.0 copy-done.11
  136.5 7.2 %shard_map.133 = (bf16[256,1024]{1,0:T(8,128)(2,1)S(1)}, bf16[256,1024]{1,0:T(8,128)(2,1)S(1)}) custom-call(bf16[256,1024]{1,0:T(8,128)(2,1)S(1)} %copy-done.11, bf16[256,1024]{1,0:T(8,128)(2,1)S(1)} %copy-done.5, bf16[1024,4096]{1,0:T(8,128)(2,1)} %all-gather.3.cloned.1.call-done.weights_hbm), custom_call_target="tpu_custom_call" | custom-call | tf_op jit(solution)/shard_map/pallas_call | solution.py:372
  143.7 3.2 %collective-permute-start.2 = (bf16[256,1024]{1,0:T(8,128)(2,1)S(1)}, bf16[256,1024]{1,0:T(8,128)(2,1)S(1)}, u32[]{:S(2)}, u32[]{:S(2)}) collective-permute-start(bf16[256,1024]{1,0:T(8,128)(2,1)S(1)} %get-tuple-element.18.refs_4_), channel_id=1, source_target_pairs={{0,1},{1,0},{2,3},{3,2},{4,5},{5,4},{6,7},{7,6},{8,9},{9,8},{10,11... | collective-permute-start | bytes 1572872 | tf_op jit(solution)/shard_map/ppermute | solution.py:392
  146.9 2.3 %collective-permute-start.1 = (bf16[256,1024]{1,0:T(8,128)(2,1)S(1)}, bf16[256,1024]{1,0:T(8,128)(2,1)S(1)}, u32[]{:S(2)}, u32[]{:S(2)}) collective-permute-start(bf16[256,1024]{1,0:T(8,128)(2,1)S(1)} %get-tuple-element.17), channel_id=1, source_target_pairs={{0,1},{1,0},{2,3},{3,2},{4,5},{5,4},{6,7},{7,6},{8,9},{9,8},{10,11... | collective-permute-start | bytes 1572872 | tf_op jit(solution)/shard_map/ppermute | solution.py:393
  149.2 9.7 %collective-permute-done.2.refs_5_ = bf16[256,1024]{1,0:T(8,128)(2,1)S(1)} collective-permute-done((bf16[256,1024]{1,0:T(8,128)(2,1)S(1)}, bf16[256,1024]{1,0:T(8,128)(2,1)S(1)}, u32[]{:S(2)}, u32[]{:S(2)}) %collective-permute-start.2) | collective-permute-done | bytes 524320 | tf_op jit(solution)/shard_map/ppermute | solution.py:392
  159.0 12.4 %shard_map.134 = f32[256,768]{1,0:T(8,128)} custom-call(bf16[16,32,4096]{2,1,0:T(8,128)(2,1)} %all_to_all.5.refs_2_.refs_0_, bf16[16,32,4096]{2,1,0:T(8,128)(2,1)} %bitcast.6.refs_3_.refs_1_, bf16[256,1024]{1,0:T(8,128)(2,1)S(1)} %copy-done.5, f32[256,1024]{1,0:T(8,128)S(1)} %copy-done.3, bf16[256,1024]{1,0:T(8,128)(2,1)S(1)} %get-tuple-element.18.refs_4_, ...), custom_call_target="tpu_custom_call" | custom-call | flops 4294967296 | bytes 20971520 | tf_op jit(solution)/shard_map/pallas_call | solution.py:397
  171.3 1.0 add_convert_fusion
  (40 shorter events, 0.8 us)
Async XLA Ops:
  7.2 128.2 %all-gather.3.cloned.1.call-start = ((), (), s32[]{:S(2)}) async-start(), calls=%async_computation.1 | async-start | bytes 8650752 | tf_op jit(solution)/shard_map/all_gather | solution.py:314
  46.1 66.0 %copy-start.16 = (s32[1,256]{1,0:T(1,128)S(1)}, s32[1,256]{1,0:T(1,128)}, u32[]{:S(2)}) copy-start(s32[1,256]{1,0:T(1,128)} %refs_6_.1) | copy-start | bytes 3076
  46.1 66.8 %copy-start = (bf16[768,1024]{1,0:T(8,128)(2,1)S(1)}, bf16[768,1024]{1,0:T(8,128)(2,1)}, u32[]{:S(2)}) copy-start(bf16[768,1024]{1,0:T(8,128)(2,1)} %refs_10_.1) | copy-start | bytes 4718596
  46.1 66.7 %copy-start.4 = (f32[256,768]{1,0:T(8,128)S(1)}, f32[256,768]{1,0:T(8,128)}, u32[]{:S(2)}) copy-start(f32[256,768]{1,0:T(8,128)} %refs_11_.1) | copy-start | bytes 2359300
  46.1 66.7 %copy-start.10 = (f32[256,768]{1,0:T(8,128)S(1)}, f32[256,768]{1,0:T(8,128)}, u32[]{:S(2)}) copy-start(f32[256,768]{1,0:T(8,128)} %pix_ref.1) | copy-start | bytes 2359300
  46.1 66.7 %copy-start.14 = (f32[1024]{0:T(1024)S(1)}, f32[1024]{0:T(1024)}, u32[]{:S(2)}) copy-start(f32[1024]{0:T(1024)} %param.17) | copy-start | bytes 12292
  101.4 18.1 %collective-permute-start = (bf16[512,4096]{1,0:T(8,128)(2,1)}, bf16[512,4096]{1,0:T(8,128)(2,1)}, u32[]{:S(2)}, u32[]{:S(2)}) collective-permute-start(bf16[512,4096]{1,0:T(8,128)(2,1)} %bitcast.5), channel_id=1, source_target_pairs={{0,16},{16,0},{32,48},{48,32},{64,80},{80,64},{96,112},{112,96},{1... | collective-permute-start | bytes 12582920 | tf_op jit(solution)/shard_map/ppermute | solution.py:321
  113.7 1.0 copy-start.1
  114.7 0.8 copy-start.12
  119.5 15.9 %copy-start.5 = (bf16[256,1024]{1,0:T(8,128)(2,1)S(1)}, bf16[256,1024]{1,0:T(8,128)(2,1)}, u32[]{:S(2)}) copy-start(bf16[256,1024]{1,0:T(8,128)(2,1)} %refs_2_.1) | copy-start | bytes 1572868
  135.4 1.0 copy-start.11
  136.5 22.4 %copy-start.2 = (f32[256,1024]{1,0:T(8,128)S(1)}, f32[256,1024]{1,0:T(8,128)}, u32[]{:S(2)}) copy-start(f32[256,1024]{1,0:T(8,128)} %copy-done.1) | copy-start | bytes 3145732
  136.5 22.4 %copy-start.3 = (f32[256,1024]{1,0:T(8,128)S(1)}, f32[256,1024]{1,0:T(8,128)}, u32[]{:S(2)}) copy-start(f32[256,1024]{1,0:T(8,128)} %get-tuple-element.15.refs_3_) | copy-start | bytes 3145732
  136.5 22.4 %copy-start.6 = (bf16[16,256,256]{2,1,0:T(8,128)(2,1)S(1)}, bf16[16,256,256]{2,1,0:T(8,128)(2,1)}, u32[]{:S(2)}) copy-start(bf16[16,256,256]{2,1,0:T(8,128)(2,1)} %get-tuple-element.20.refs_7_) | copy-start | bytes 6291460
  136.5 22.4 %copy-start.7 = (bf16[16,256,256]{2,1,0:T(8,128)(2,1)S(1)}, bf16[16,256,256]{2,1,0:T(8,128)(2,1)}, u32[]{:S(2)}) copy-start(bf16[16,256,256]{2,1,0:T(8,128)(2,1)} %get-tuple-element.21.refs_8_) | copy-start | bytes 6291460
  136.5 22.4 %copy-start.8 = (bf16[3,256,1024]{2,1,0:T(8,128)(2,1)S(1)}, bf16[3,256,1024]{2,1,0:T(8,128)(2,1)}, u32[]{:S(2)}) copy-start(bf16[3,256,1024]{2,1,0:T(8,128)(2,1)} %get-tuple-element.19.refs_6_) | copy-start | bytes 4718596
  136.5 22.4 %copy-start.9 = (s32[256,1]{1,0:T(8,128)S(1)}, s32[256,1]{1,0:T(8,128)}, u32[]{:S(2)}) copy-start(s32[256,1]{1,0:T(8,128)} %copy.19.refs_5_.refs_15_) | copy-start | bytes 3076
  136.5 22.4 %copy-start.13 = (f32[1024]{0:T(1024)S(1)}, f32[1024]{0:T(1024)}, u32[]{:S(2)}) copy-start(f32[1024]{0:T(1024)} %param.20) | copy-start | bytes 12292
  136.5 22.4 %copy-start.15 = (f32[1,4]{1,0:T(1,128)S(1)}, f32[1,4]{1,0:T(1,128)}, u32[]{:S(2)}) copy-start(f32[1,4]{1,0:T(1,128)} %refs_14_.1) | copy-start | bytes 52
  143.7 15.2 %collective-permute-start.2 = (bf16[256,1024]{1,0:T(8,128)(2,1)S(1)}, bf16[256,1024]{1,0:T(8,128)(2,1)S(1)}, u32[]{:S(2)}, u32[]{:S(2)}) collective-permute-start(bf16[256,1024]{1,0:T(8,128)(2,1)S(1)} %get-tuple-element.18.refs_4_), channel_id=1, source_target_pairs={{0,1},{1,0},{2,3},{3,2},{4,5},{5,4},{6,7},{7,6},{8,9},{9,8},{10,11... | collective-permute-start | bytes 1572872 | tf_op jit(solution)/shard_map/ppermute | solution.py:392
  146.9 24.4 %collective-permute-start.1 = (bf16[256,1024]{1,0:T(8,128)(2,1)S(1)}, bf16[256,1024]{1,0:T(8,128)(2,1)S(1)}, u32[]{:S(2)}, u32[]{:S(2)}) collective-permute-start(bf16[256,1024]{1,0:T(8,128)(2,1)S(1)} %get-tuple-element.17), channel_id=1, source_target_pairs={{0,1},{1,0},{2,3},{3,2},{4,5},{5,4},{6,7},{7,6},{8,9},{9,8},{10,11... | collective-permute-start | bytes 1572872 | tf_op jit(solution)/shard_map/ppermute | solution.py:393
Sparse Core Ops, SparseCore 0:
  44.4 91.0 all-gather.2

commit v6 on v5

--- a/solution.py
+++ b/solution.py
@@ -135,7 +135,7 @@
 
 
 def mlp_kernel(
-    n2_hbm, og_hbm, weights_hbm, up_ref, out_ref,
+    n2_hbm, og_hbm, weights_hbm, top_ref, low_ref, out_ref,
     n2_ref, og_ref, up_buf, down_buf, acc_out, acc_grad, up_sem, down_sem, sem,
 ):
     chunks, _, width = up_buf.shape
@@ -186,36 +186,31 @@
         later = front(j + 1) if j + 1 < chunks else None
         back(j, *now)
         now = later
-    up_ref[...] = acc_grad[...].astype(BF16)
+    middle = top_ref.shape[0]
+    top_ref[...] = acc_grad[:middle].astype(BF16)
+    low_ref[...] = acc_grad[middle:].astype(BF16)
     out_ref[...] = acc_out[...].astype(BF16)
 
 
 def backward_kernel(
     size, images,
-    near_hbm, far_hbm,
-    og_ref, mid_ref, mine_ref, theirs_ref, qkv_buf, low_buf, turned_buf,
+    attn_buf,
+    og_ref, mid_ref, top_mine_ref, top_theirs_ref, low_mine_ref, low_theirs_ref, qkv_buf, low_buf, turned_buf,
     emb_ref, emb_w_ref, pert_ref, gain1_ref, gain2_ref, ball_ref, col_ref,
     new_ref,
-    attn_buf, acc_grad, heads_ref, proj_ref, sem,
+    acc_grad, heads_ref, proj_ref,
 ):
     rows, model = og_ref.shape
-    core = lax.rem(lax.axis_index("rows"), 2)
-    head_part = pl.ds(0, 3 * model)
-    out_part = pl.ds(3 * model, model)
-    pairs = (
-        (near_hbm.at[:, :, out_part], attn_buf.at[:, core, :, out_part]),
-        (far_hbm.at[:, :, out_part], attn_buf.at[:, 1 - core, :, out_part]),
-        (near_hbm.at[:, :, head_part], attn_buf.at[:, core, :, head_part]),
-        (far_hbm.at[:, :, head_part], attn_buf.at[:, 1 - core, :, head_part]),
-    )
-    copies = [pltpu.make_async_copy(*pair, sem.at[i]) for i, pair in enumerate(pairs)]
-    for copy in copies:
-        copy.start()
-    grad_norm_two = mine_ref[...].astype(F32) + theirs_ref[...].astype(F32)
-    grad_mid = og_ref[...].astype(F32) + norm_back(mid_ref[...], gain2_ref[...], grad_norm_two)
-    acc_grad[...] = grad_mid
-    for copy in copies[:2]:
-        copy.wait()
+    middle = rows // 2
+    for part, mine, theirs in (
+        (slice(0, middle), top_mine_ref, top_theirs_ref),
+        (slice(middle, rows), low_mine_ref, low_theirs_ref),
+    ):
+        grad_norm_two = mine[...].astype(F32) + theirs[...].astype(F32)
+        acc_grad[part] = og_ref[part].astype(F32) + norm_back(
+            mid_ref[part], gain2_ref[...], grad_norm_two
+        )
+    grad_mid = acc_grad[...]
     heads_ref[...] = mm(grad_mid.astype(BF16), columns(attn_buf, 3, 4)).astype(BF16)
     quad = 4 * size
     scale = 1.0 / math.sqrt(size)
@@ -243,8 +238,6 @@
         return carry
 
     lax.fori_loop(0, model // quad, attention_step, 0)
-    for copy in copies[2:]:
-        copy.wait()
     grad_norm = mm_nt(proj_ref[...], columns(attn_buf, 0, 3))
     grad_embed = acc_grad[...] + norm_back(emb_ref[...], gain1_ref[...], grad_norm)
     grad_input = mm_nt(grad_embed.astype(BF16), emb_w_ref[...])
@@ -273,6 +266,16 @@
     new_ref[...] = candidate * factor_rows
 
 
+def place_kernel(near_hbm, far_hbm, placed_ref, sem):
+    core = lax.rem(lax.axis_index("rows"), 2)
+    first = pltpu.make_async_copy(near_hbm, placed_ref.at[:, core], sem.at[0])
+    second = pltpu.make_async_copy(far_hbm, placed_ref.at[:, 1 - core], sem.at[1])
+    first.start()
+    second.start()
+    first.wait()
+    second.wait()
+
+
 def block(*shape, dtype=BF16):
     return pltpu.VMEM(shape, dtype)
 
@@ -369,11 +372,12 @@
 
     width = 1024
     count = groups * units // 2 // width
-    up_mine, out_mine = pl.pallas_call(
+    half_rows = jax.ShapeDtypeStruct((rows // 2, model), BF16)
+    top_mine, low_mine, out_mine = pl.pallas_call(
         mlp_kernel,
         in_specs=[outside] * 3,
-        out_specs=[vmem] * 2,
-        out_shape=[full(BF16), full(BF16)],
+        out_specs=[vmem] * 3,
+        out_shape=[half_rows, half_rows, full(BF16)],
         scratch_shapes=[
             block(rows, model),
             block(rows, model),
@@ -388,29 +392,40 @@
         compiler_params=params(49),
     )(normed_two, out_grad, weights)
 
-    pairs = [(group, group ^ 1) for group in range(groups)]
-    up_theirs = lax.ppermute(up_mine, "heads", pairs)
-    out_theirs = lax.ppermute(out_mine, "heads", pairs)
-
-    held = (out_grad, stream_mid, up_mine, up_theirs, qkv, low, turned, embedded, w_embed)
+    down = [(group, (group - 1) % groups) for group in range(groups)]
+    above = [(group, (group + 1) % groups) for group in range(groups)]
+    top_theirs = lax.ppermute(top_mine, "heads", down)
+    low_theirs = lax.ppermute(low_mine, "heads", above)
+    out_theirs = lax.ppermute(out_mine, "heads", [(group, group ^ 1) for group in range(groups)])
+    near, far, _ = lax.optimization_barrier((near, far, top_mine))
+    placed = pl.pallas_call(
+        place_kernel,
+        in_specs=[outside] * 2,
+        out_specs=vmem,
+        out_shape=jax.ShapeDtypeStruct((sites, 2, chunk, 4 * model), BF16),
+        scratch_shapes=[semaphores((2,))],
+        compiler_params=params(20),
+        cost_estimate=pl.CostEstimate(flops=0, bytes_accessed=8 * MIB, transcendentals=0),
+    )(near, far)
+
+    held = (placed, out_grad, stream_mid, top_mine, top_theirs, low_mine, low_theirs)
+    held = held + (qkv, low, turned, embedded, w_embed)
     held = held + (perturbation, gain1, gain2, ball_radius, labels_col)
     updated = pl.pallas_call(
         lambda *refs: backward_kernel(size, images, *refs),
-        in_specs=[outside] * 2 + [vmem] * len(held),
+        in_specs=[vmem] * len(held),
         out_specs=vmem,
         out_shape=jax.ShapeDtypeStruct((rows, patch), F32),
         scratch_shapes=[
-            block(sites, 2, chunk, 4 * model),
             block(rows, model, dtype=F32),
             block(rows, model),
             block(rows, 3 * model),
-            semaphores((4,)),
         ],
-        compiler_params=params(30),
+        compiler_params=params(24),
         cost_estimate=pl.CostEstimate(
             flops=16 * rows * model * model, bytes_accessed=20 * 1024 * 1024, transcendentals=0
         ),
-    )(near, far, *held)
+    )(*held)
     out_theirs, updated = lax.optimization_barrier((out_theirs, updated))
     block_out = stream_mid + (out_mine.astype(F32) + out_theirs.astype(F32))
     return (block_out.astype(BF16), updated)

time: 180 us -> 177 us (0.983)
  waiting for transfers between devices: 18.5 us -> 8.87 us
  starting transfers between devices: 16.2 us -> 20.8 us
  Pallas kernels: 31.5 us -> 34 us
    ppermute x2 -> x3, waiting for transfers between devices: 9.69 us -> 0.01 us  [the longest x1 0.01 us: body(): low_theirs = lax.ppermute(low_mine, 'heads', above)]
    ppermute x2 -> x3, starting transfers between devices: 5.46 us -> 10.1 us  [the longest x1 4.41 us: body(): top_theirs = lax.ppermute(top_mine, 'heads', down)]
    pallas_call x1 -> x2, Pallas kernels: 7.21 us -> 10.6 us  [the longest x1 7.06 us: body(): pl.pallas_call(mlp_kernel, in_specs=[outside] * 3, out_specs=[vmem] * 3,...]
  transfers between devices with their start and end apart: 4 -> 5, of which waited for: 3 -> 2; matrix products, arithmetic and copies ran while one was open for 1% -> 1% of each run, Pallas kernels for 14% -> 15%
where the time goes in v6:
time: 177 us
  blocking collectives  89.1 us (50%)
  Pallas kernels  34 us (19%)
  starting transfers between devices  20.8 us (12%)
  between operations  14.4 us (8%)
  waiting for transfers between devices  8.87 us (5%)
  local copies, waits for them, and re-layouts  7.76 us (4%)
  other arithmetic  1.87 us (1%)
    all_to_all x1, blocking collectives, body(): near = lax.all_to_all(copies, 'rows', 0, 0, axis_index_groups=planes)  55.2 us
    all_gather x1, blocking collectives, body(): chunks = lax.all_gather(mine, 'heads', axis=0, tiled=False)  33.9 us
    pallas_call x1, Pallas kernels, body(): pl.pallas_call(lambda *refs: backward_kernel(size, images, *refs), in_spe...  11.6 us
    pallas_call x1, Pallas kernels, body(): pl.pallas_call(lambda *refs: attention_kernel(size, *refs), in_specs=[out...  11.1 us
    ppermute x1, starting transfers between devices, body(): lax.ppermute(near, 'rows', [(row, row ^ 1) for row in range(2 * sites)])  10.7 us
    pallas_call x1, Pallas kernels, body(): pl.pallas_call(mlp_kernel, in_specs=[outside] * 3, out_specs=[vmem] * 3,...  7.06 us
    all_gather x1, waiting for transfers between devices, body(): weights = lax.all_gather(mlp, 'rows', axis=0, tiled=True)  4.82 us
    unnamed x37, local copies, waits for them, and re-layouts  4.69 us
  transfers between devices with their start and end apart: 5, of which 2 were waited for; matrix products, arithmetic and copies ran while one was open for 1% of the time, Pallas kernels for 15%

profile of v6, /device:TPU:1, one launch (start us, length us, event | category | flops | bytes accessed | tf_op | source)
XLA Modules:
  0.0 176.8 jit_solution(379744230430261308)
XLA Ops:
  7.2 0.8 copy.17
  8.1 0.8 pad_maximum_fusion
  8.9 33.9 %all-gather = bf16[512,768]{1,0:T(8,128)(2,1)S(1)} all-gather(bf16[32,768]{1,0:T(8,128)(2,1)S(1)} %pad_maximum_fusion), channel_id=2, replica_groups=mesh['rows'=32,'heads'=16] {'heads'}, dimensions={0}, use_global_device_ids=true | all-gather | bytes 835584 | tf_op jit(solution)/shard_map/all_gather | solution.py:310
  43.4 0.8 copy.23
  44.5 0.6 copy.25
  45.1 0.5 broadcast_in_dim.7
  45.6 0.5 broadcast_in_dim.8
  46.2 55.2 %all_to_all.5.refs_2_.near_hbm = bf16[16,32,4096]{2,1,0:T(8,128)(2,1)} all-to-all(bf16[16,32,4096]{2,1,0:T(8,128)(2,1)S(1)} %broadcast_in_dim.8), channel_id=1, replica_groups={{0,32,64,96,128,160,192,224,256,288,320,352,384,416,448,480},{16,48,80,..., dimensions={0} | all-to-all | bytes 8388608 | tf_op jit(solution)/shard_map/all_to_all | solution.py:322
  101.4 10.7 %collective-permute-start = (bf16[512,4096]{1,0:T(8,128)(2,1)}, bf16[512,4096]{1,0:T(8,128)(2,1)}, u32[]{:S(2)}, u32[]{:S(2)}) collective-permute-start(bf16[512,4096]{1,0:T(8,128)(2,1)} %bitcast.5), channel_id=1, source_target_pairs={{0,16},{16,0},{32,48},{48,32},{64,80},{80,64},{96,112},{112,96},{1... | collective-permute-start | bytes 12582920 | tf_op jit(solution)/shard_map/ppermute | solution.py:324
  112.1 0.8 copy.19.refs_5_.refs_16_
  112.9 0.8 shard_map.131
  113.7 1.0 copy-done.1
  114.7 0.8 copy-done.12
  115.5 4.0 %collective-permute-done = bf16[512,4096]{1,0:T(8,128)(2,1)} collective-permute-done((bf16[512,4096]{1,0:T(8,128)(2,1)}, bf16[512,4096]{1,0:T(8,128)(2,1)}, u32[]{:S(2)}, u32[]{:S(2)}) %collective-permute-start) | collective-permute-done | bytes 4194336 | tf_op jit(solution)/shard_map/ppermute | solution.py:324
  119.5 11.1 %shard_map.132 = (bf16[3,256,1024]{2,1,0:T(8,128)(2,1)}, bf16[16,256,256]{2,1,0:T(8,128)(2,1)}, bf16[16,256,256]{2,1,0:T(8,128)(2,1)}, f32[256,1024]{1,0:T(8,128)}, bf16[256,1024]{1,0:T(8,128)(2,1)}) custom-call(bf16[256,1024]{1,0:T(8,128)(2,1)} %copy-done.12, f32[256,1024]{1,0:T(8,128)} %copy-done.1, bf16[16,32,4096]{2,1,0:T(8,128)(2,1)} %all_to_all.5.refs_2_.near_hbm, ...), custom_call_target="tpu_custom_call" | custom-call | tf_op jit(solution)/shard_map/pallas_call | solution.py:351
  130.6 4.8 %all-gather.3.cloned.1.call-done.weights_hbm = bf16[1024,4096]{1,0:T(8,128)(2,1)} async-done(((bf16[32,4096]{1,0:T(8,128)(2,1)}), bf16[1024,4096]{1,0:T(8,128)(2,1)}) %all-gather.3.cloned.1.call-update) | async-done | bytes 8388624 | tf_op jit(solution)/shard_map/all_gather | solution.py:317
  135.4 1.0 copy-done.11
  136.5 7.1 %shard_map.133 = (bf16[128,1024]{1,0:T(8,128)(2,1)S(1)}, bf16[128,1024]{1,0:T(8,128)(2,1)S(1)}, bf16[256,1024]{1,0:T(8,128)(2,1)S(1)}) custom-call(bf16[256,1024]{1,0:T(8,128)(2,1)S(1)} %copy-done.11, bf16[256,1024]{1,0:T(8,128)(2,1)S(1)} %copy-done.5, bf16[1024,4096]{1,0:T(8,128)(2,1)} %all-gather.3.cloned.1.call-done.weights_hbm), custom_call_target="tpu_custom_call" | custom-call | tf_op jit(solution)/shard_map/pallas_call | solution.py:376
  143.5 3.2 %collective-permute-start.3 = (bf16[128,1024]{1,0:T(8,128)(2,1)S(1)}, bf16[128,1024]{1,0:T(8,128)(2,1)S(1)}, u32[]{:S(2)}, u32[]{:S(2)}) collective-permute-start(bf16[128,1024]{1,0:T(8,128)(2,1)S(1)} %get-tuple-element.24.refs_5_), channel_id=1, source_target_pairs={{0,1},{1,2},{2,3},{3,4},{4,5},{5,6},{6,7},{7,8},{8,9},{9,10},{10,1... | collective-permute-start | bytes 786440 | tf_op jit(solution)/shard_map/ppermute | solution.py:398
  146.7 4.4 %collective-permute-start.2 = (bf16[128,1024]{1,0:T(8,128)(2,1)S(1)}, bf16[128,1024]{1,0:T(8,128)(2,1)S(1)}, u32[]{:S(2)}, u32[]{:S(2)}) collective-permute-start(bf16[128,1024]{1,0:T(8,128)(2,1)S(1)} %get-tuple-element.21.refs_3_), channel_id=1, source_target_pairs={{0,15},{1,0},{2,1},{3,2},{4,3},{5,4},{6,5},{7,6},{8,7},{9,8},{10,9... | collective-permute-start | bytes 786440 | tf_op jit(solution)/shard_map/ppermute | solution.py:397
  151.2 2.5 %collective-permute-start.1 = (bf16[256,1024]{1,0:T(8,128)(2,1)S(1)}, bf16[256,1024]{1,0:T(8,128)(2,1)S(1)}, u32[]{:S(2)}, u32[]{:S(2)}) collective-permute-start(bf16[256,1024]{1,0:T(8,128)(2,1)S(1)} %get-tuple-element.20), channel_id=1, source_target_pairs={{0,1},{1,0},{2,3},{3,2},{4,5},{5,4},{6,7},{7,6},{8,9},{9,8},{10,11... | collective-permute-start | bytes 1572872 | tf_op jit(solution)/shard_map/ppermute | solution.py:399
  153.7 3.5 %shard_map.134.refs_0_ = bf16[16,2,32,4096]{3,2,1,0:T(8,128)(2,1)S(1)} custom-call(bf16[16,32,4096]{2,1,0:T(8,128)(2,1)} %all_to_all.5.refs_2_.near_hbm, bf16[16,32,4096]{2,1,0:T(8,128)(2,1)} %bitcast.6.refs_3_.far_hbm), custom_call_target="tpu_custom_call" | custom-call | bytes 8388608 | tf_op jit(solution)/shard_map/pallas_call | solution.py:401
  157.3 11.6 %shard_map.135 = f32[256,768]{1,0:T(8,128)} custom-call(bf16[16,2,32,4096]{3,2,1,0:T(8,128)(2,1)S(1)} %shard_map.134.refs_0_, bf16[256,1024]{1,0:T(8,128)(2,1)S(1)} %copy-done.5, f32[256,1024]{1,0:T(8,128)S(1)} %copy-done.3, bf16[128,1024]{1,0:T(8,128)(2,1)S(1)} %get-tuple-element.21.refs_3_, bf16[128,1024]{1,0:T(8,128)(2,1)S(1)} %collective-permute-done.2.refs_4_, ...), custom_call_target="tpu_custom_call" | custom-call | flops 4294967296 | bytes 20971520 | tf_op jit(solution)/shard_map/pallas_call | solution.py:414
  168.9 1.1 add_convert_fusion
  (43 shorter events, 1.1 us)
Async XLA Ops:
  7.2 128.2 %all-gather.3.cloned.1.call-start = ((), (), s32[]{:S(2)}) async-start(), calls=%async_computation.1 | async-start | bytes 8650752 | tf_op jit(solution)/shard_map/all_gather | solution.py:317
  46.1 66.0 %copy-start.16 = (s32[1,256]{1,0:T(1,128)S(1)}, s32[1,256]{1,0:T(1,128)}, u32[]{:S(2)}) copy-start(s32[1,256]{1,0:T(1,128)} %refs_6_.1) | copy-start | bytes 3076
  46.1 66.8 %copy-start = (bf16[768,1024]{1,0:T(8,128)(2,1)S(1)}, bf16[768,1024]{1,0:T(8,128)(2,1)}, u32[]{:S(2)}) copy-start(bf16[768,1024]{1,0:T(8,128)(2,1)} %refs_11_.1) | copy-start | bytes 4718596
  46.1 66.7 %copy-start.4 = (f32[256,768]{1,0:T(8,128)S(1)}, f32[256,768]{1,0:T(8,128)}, u32[]{:S(2)}) copy-start(f32[256,768]{1,0:T(8,128)} %refs_12_.1) | copy-start | bytes 2359300
  46.1 66.7 %copy-start.10 = (f32[256,768]{1,0:T(8,128)S(1)}, f32[256,768]{1,0:T(8,128)}, u32[]{:S(2)}) copy-start(f32[256,768]{1,0:T(8,128)} %pix_ref.1) | copy-start | bytes 2359300
  46.1 66.7 %copy-start.14 = (f32[1024]{0:T(1024)S(1)}, f32[1024]{0:T(1024)}, u32[]{:S(2)}) copy-start(f32[1024]{0:T(1024)} %param.17) | copy-start | bytes 12292
  101.4 18.1 %collective-permute-start = (bf16[512,4096]{1,0:T(8,128)(2,1)}, bf16[512,4096]{1,0:T(8,128)(2,1)}, u32[]{:S(2)}, u32[]{:S(2)}) collective-permute-start(bf16[512,4096]{1,0:T(8,128)(2,1)} %bitcast.5), channel_id=1, source_target_pairs={{0,16},{16,0},{32,48},{48,32},{64,80},{80,64},{96,112},{112,96},{1... | collective-permute-start | bytes 12582920 | tf_op jit(solution)/shard_map/ppermute | solution.py:324
  113.7 1.0 copy-start.1
  114.7 0.8 copy-start.12
  119.5 15.9 %copy-start.5 = (bf16[256,1024]{1,0:T(8,128)(2,1)S(1)}, bf16[256,1024]{1,0:T(8,128)(2,1)}, u32[]{:S(2)}) copy-start(bf16[256,1024]{1,0:T(8,128)(2,1)} %refs_1_.1) | copy-start | bytes 1572868
  135.4 1.0 copy-start.11
  143.5 13.7 %collective-permute-start.3 = (bf16[128,1024]{1,0:T(8,128)(2,1)S(1)}, bf16[128,1024]{1,0:T(8,128)(2,1)S(1)}, u32[]{:S(2)}, u32[]{:S(2)}) collective-permute-start(bf16[128,1024]{1,0:T(8,128)(2,1)S(1)} %get-tuple-element.24.refs_5_), channel_id=1, source_target_pairs={{0,1},{1,2},{2,3},{3,4},{4,5},{5,6},{6,7},{7,8},{8,9},{9,10},{10,1... | collective-permute-start | bytes 786440 | tf_op jit(solution)/shard_map/ppermute | solution.py:398
  146.7 10.5 %collective-permute-start.2 = (bf16[128,1024]{1,0:T(8,128)(2,1)S(1)}, bf16[128,1024]{1,0:T(8,128)(2,1)S(1)}, u32[]{:S(2)}, u32[]{:S(2)}) collective-permute-start(bf16[128,1024]{1,0:T(8,128)(2,1)S(1)} %get-tuple-element.21.refs_3_), channel_id=1, source_target_pairs={{0,15},{1,0},{2,1},{3,2},{4,3},{5,4},{6,5},{7,6},{8,7},{9,8},{10,9... | collective-permute-start | bytes 786440 | tf_op jit(solution)/shard_map/ppermute | solution.py:397
  151.1 6.1 %copy-start.2 = (f32[256,1024]{1,0:T(8,128)S(1)}, f32[256,1024]{1,0:T(8,128)}, u32[]{:S(2)}) copy-start(f32[256,1024]{1,0:T(8,128)} %copy-done.1) | copy-start | bytes 3145732
  151.1 6.1 %copy-start.3 = (f32[256,1024]{1,0:T(8,128)S(1)}, f32[256,1024]{1,0:T(8,128)}, u32[]{:S(2)}) copy-start(f32[256,1024]{1,0:T(8,128)} %get-tuple-element.18.refs_2_) | copy-start | bytes 3145732
  151.2 6.1 %copy-start.6 = (bf16[16,256,256]{2,1,0:T(8,128)(2,1)S(1)}, bf16[16,256,256]{2,1,0:T(8,128)(2,1)}, u32[]{:S(2)}) copy-start(bf16[16,256,256]{2,1,0:T(8,128)(2,1)} %get-tuple-element.26.refs_8_) | copy-start | bytes 6291460
  151.2 6.1 %copy-start.7 = (bf16[16,256,256]{2,1,0:T(8,128)(2,1)S(1)}, bf16[16,256,256]{2,1,0:T(8,128)(2,1)}, u32[]{:S(2)}) copy-start(bf16[16,256,256]{2,1,0:T(8,128)(2,1)} %get-tuple-element.27.refs_9_) | copy-start | bytes 6291460
  151.2 6.1 %copy-start.8 = (bf16[3,256,1024]{2,1,0:T(8,128)(2,1)S(1)}, bf16[3,256,1024]{2,1,0:T(8,128)(2,1)}, u32[]{:S(2)}) copy-start(bf16[3,256,1024]{2,1,0:T(8,128)(2,1)} %get-tuple-element.25.refs_7_) | copy-start | bytes 4718596
  151.2 6.1 %copy-start.9 = (s32[256,1]{1,0:T(8,128)S(1)}, s32[256,1]{1,0:T(8,128)}, u32[]{:S(2)}) copy-start(s32[256,1]{1,0:T(8,128)} %copy.19.refs_5_.refs_16_) | copy-start | bytes 3076
  151.2 6.1 %copy-start.13 = (f32[1024]{0:T(1024)S(1)}, f32[1024]{0:T(1024)}, u32[]{:S(2)}) copy-start(f32[1024]{0:T(1024)} %param.20) | copy-start | bytes 12292
  151.2 6.1 %copy-start.15 = (f32[1,4]{1,0:T(1,128)S(1)}, f32[1,4]{1,0:T(1,128)}, u32[]{:S(2)}) copy-start(f32[1,4]{1,0:T(1,128)} %refs_15_.1) | copy-start | bytes 52
  151.2 17.7 %collective-permute-start.1 = (bf16[256,1024]{1,0:T(8,128)(2,1)S(1)}, bf16[256,1024]{1,0:T(8,128)(2,1)S(1)}, u32[]{:S(2)}, u32[]{:S(2)}) collective-permute-start(bf16[256,1024]{1,0:T(8,128)(2,1)S(1)} %get-tuple-element.20), channel_id=1, source_target_pairs={{0,1},{1,0},{2,3},{3,2},{4,5},{5,4},{6,7},{7,6},{8,9},{9,8},{10,11... | collective-permute-start | bytes 1572872 | tf_op jit(solution)/shard_map/ppermute | solution.py:399
Sparse Core Ops, SparseCore 0:
  44.4 91.0 all-gather.2

commit v7 on v5

--- a/solution.py
+++ b/solution.py
@@ -135,7 +135,7 @@
 
 
 def mlp_kernel(
-    n2_hbm, og_hbm, weights_hbm, up_ref, out_ref,
+    n2_hbm, og_hbm, weights_hbm, top_ref, low_ref, out_ref,
     n2_ref, og_ref, up_buf, down_buf, acc_out, acc_grad, up_sem, down_sem, sem,
 ):
     chunks, _, width = up_buf.shape
@@ -186,14 +186,16 @@
         later = front(j + 1) if j + 1 < chunks else None
         back(j, *now)
         now = later
-    up_ref[...] = acc_grad[...].astype(BF16)
+    middle = top_ref.shape[0]
+    top_ref[...] = acc_grad[:middle].astype(BF16)
+    low_ref[...] = acc_grad[middle:].astype(BF16)
     out_ref[...] = acc_out[...].astype(BF16)
 
 
 def backward_kernel(
     size, images,
     near_hbm, far_hbm,
-    og_ref, mid_ref, mine_ref, theirs_ref, qkv_buf, low_buf, turned_buf,
+    og_ref, mid_ref, top_mine_ref, top_theirs_ref, low_mine_ref, low_theirs_ref, qkv_buf, low_buf, turned_buf,
     emb_ref, emb_w_ref, pert_ref, gain1_ref, gain2_ref, ball_ref, col_ref,
     new_ref,
     attn_buf, acc_grad, heads_ref, proj_ref, sem,
@@ -211,9 +213,16 @@
     copies = [pltpu.make_async_copy(*pair, sem.at[i]) for i, pair in enumerate(pairs)]
     for copy in copies:
         copy.start()
-    grad_norm_two = mine_ref[...].astype(F32) + theirs_ref[...].astype(F32)
-    grad_mid = og_ref[...].astype(F32) + norm_back(mid_ref[...], gain2_ref[...], grad_norm_two)
-    acc_grad[...] = grad_mid
+    middle = rows // 2
+    for part, mine, theirs in (
+        (slice(0, middle), top_mine_ref, top_theirs_ref),
+        (slice(middle, rows), low_mine_ref, low_theirs_ref),
+    ):
+        grad_norm_two = mine[...].astype(F32) + theirs[...].astype(F32)
+        acc_grad[part] = og_ref[part].astype(F32) + norm_back(
+            mid_ref[part], gain2_ref[...], grad_norm_two
+        )
+    grad_mid = acc_grad[...]
     for copy in copies[:2]:
         copy.wait()
     heads_ref[...] = mm(grad_mid.astype(BF16), columns(attn_buf, 3, 4)).astype(BF16)
@@ -369,11 +378,12 @@
 
     width = 1024
     count = groups * units // 2 // width
-    up_mine, out_mine = pl.pallas_call(
+    half_rows = jax.ShapeDtypeStruct((rows // 2, model), BF16)
+    top_mine, low_mine, out_mine = pl.pallas_call(
         mlp_kernel,
         in_specs=[outside] * 3,
-        out_specs=[vmem] * 2,
-        out_shape=[full(BF16), full(BF16)],
+        out_specs=[vmem] * 3,
+        out_shape=[half_rows, half_rows, full(BF16)],
         scratch_shapes=[
             block(rows, model),
             block(rows, model),
@@ -388,11 +398,13 @@
         compiler_params=params(49),
     )(normed_two, out_grad, weights)
 
-    pairs = [(group, group ^ 1) for group in range(groups)]
-    up_theirs = lax.ppermute(up_mine, "heads", pairs)
-    out_theirs = lax.ppermute(out_mine, "heads", pairs)
-
-    held = (out_grad, stream_mid, up_mine, up_theirs, qkv, low, turned, embedded, w_embed)
+    down = [(group, (group - 1) % groups) for group in range(groups)]
+    above = [(group, (group + 1) % groups) for group in range(groups)]
+    top_theirs = lax.ppermute(top_mine, "heads", down)
+    low_theirs = lax.ppermute(low_mine, "heads", above)
+    out_theirs = lax.ppermute(out_mine, "heads", [(group, group ^ 1) for group in range(groups)])
+    held = (out_grad, stream_mid, top_mine, top_theirs, low_mine, low_theirs)
+    held = held + (qkv, low, turned, embedded, w_embed)
     held = held + (perturbation, gain1, gain2, ball_radius, labels_col)
     updated = pl.pallas_call(
         lambda *refs: backward_kernel(size, images, *refs),

time: 180 us -> 181 us (level)
  starting transfers between devices: 16.2 us -> 20.4 us
  waiting for transfers between devices: 18.5 us -> 15.3 us
    ppermute x2 -> x3, starting transfers between devices: 5.46 us -> 9.69 us  [the longest x1 5.67 us: body(): top_theirs = lax.ppermute(top_mine, 'heads', down)]
    ppermute x2 -> x3, waiting for transfers between devices: 9.69 us -> 6.41 us  [the longest x1 5.01 us: body(): low_theirs = lax.ppermute(low_mine, 'heads', above)]
  transfers between devices with their start and end apart: 4 -> 5, of which waited for: 3 -> 4; matrix products, arithmetic and copies ran while one was open for 1% -> 1% of each run, Pallas kernels for 14% -> 13%
where the time goes in v7:
time: 181 us; the launch traced here: 180 us
  blocking collectives  89.1 us (49%)
  Pallas kernels  31.5 us (17%)
  starting transfers between devices  20.4 us (11%)
  waiting for transfers between devices  15.3 us (8%)
  between operations  14.3 us (8%)
  local copies, waits for them, and re-layouts  7.76 us (4%)
  other arithmetic  1.85 us (1%)
    all_to_all x1, blocking collectives, body(): near = lax.all_to_all(copies, 'rows', 0, 0, axis_index_groups=planes)  55.2 us
    all_gather x1, blocking collectives, body(): chunks = lax.all_gather(mine, 'heads', axis=0, tiled=False)  33.9 us
    pallas_call x1, Pallas kernels, body(): pl.pallas_call(lambda *refs: backward_kernel(size, images, *refs), in_spe...  12.4 us
    pallas_call x1, Pallas kernels, body(): pl.pallas_call(lambda *refs: attention_kernel(size, *refs), in_specs=[out...  11.1 us
    ppermute x1, starting transfers between devices, body(): lax.ppermute(near, 'rows', [(row, row ^ 1) for row in range(2 * sites)])  10.7 us
    pallas_call x1, Pallas kernels, body(): pl.pallas_call(mlp_kernel, in_specs=[outside] * 3, out_specs=[vmem] * 3,...  7.22 us
    ppermute x1, starting transfers between devices, body(): top_theirs = lax.ppermute(top_mine, 'heads', down)  5.67 us
    ppermute x1, waiting for transfers between devices, body(): low_theirs = lax.ppermute(low_mine, 'heads', above)  5.01 us
  transfers between devices with their start and end apart: 5, of which 4 were waited for; matrix products, arithmetic and copies ran while one was open for 1% of the time, Pallas kernels for 13%

profile of v7, /device:TPU:1, one launch (start us, length us, event | category | flops | bytes accessed | tf_op | source)
XLA Modules:
  0.0 180.2 jit_solution(8614086240629072326)
XLA Ops:
  7.2 0.8 copy.17
  8.1 0.8 pad_maximum_fusion
  8.9 33.9 %all-gather = bf16[512,768]{1,0:T(8,128)(2,1)S(1)} all-gather(bf16[32,768]{1,0:T(8,128)(2,1)S(1)} %pad_maximum_fusion), channel_id=2, replica_groups=mesh['rows'=32,'heads'=16] {'heads'}, dimensions={0}, use_global_device_ids=true | all-gather | bytes 835584 | tf_op jit(solution)/shard_map/all_gather | solution.py:316
  43.4 0.8 copy.23
  44.5 0.6 copy.25
  45.6 0.5 broadcast_in_dim.8
  46.2 55.2 %all_to_all.5.refs_2_.refs_0_ = bf16[16,32,4096]{2,1,0:T(8,128)(2,1)} all-to-all(bf16[16,32,4096]{2,1,0:T(8,128)(2,1)S(1)} %broadcast_in_dim.8), channel_id=1, replica_groups={{0,32,64,96,128,160,192,224,256,288,320,352,384,416,448,480},{16,48,80,..., dimensions={0} | all-to-all | bytes 8388608 | tf_op jit(solution)/shard_map/all_to_all | solution.py:328
  101.4 10.7 %collective-permute-start = (bf16[512,4096]{1,0:T(8,128)(2,1)}, bf16[512,4096]{1,0:T(8,128)(2,1)}, u32[]{:S(2)}, u32[]{:S(2)}) collective-permute-start(bf16[512,4096]{1,0:T(8,128)(2,1)} %bitcast.5), channel_id=1, source_target_pairs={{0,16},{16,0},{32,48},{48,32},{64,80},{80,64},{96,112},{112,96},{1... | collective-permute-start | bytes 12582920 | tf_op jit(solution)/shard_map/ppermute | solution.py:330
  112.1 0.8 copy.19.refs_5_.refs_17_
  112.9 0.8 shard_map.131
  113.7 1.0 copy-done.1
  114.7 0.8 copy-done.12
  115.5 4.0 %collective-permute-done = bf16[512,4096]{1,0:T(8,128)(2,1)} collective-permute-done((bf16[512,4096]{1,0:T(8,128)(2,1)}, bf16[512,4096]{1,0:T(8,128)(2,1)}, u32[]{:S(2)}, u32[]{:S(2)}) %collective-permute-start) | collective-permute-done | bytes 4194336 | tf_op jit(solution)/shard_map/ppermute | solution.py:330
  119.5 11.1 %shard_map.132 = (bf16[3,256,1024]{2,1,0:T(8,128)(2,1)}, bf16[16,256,256]{2,1,0:T(8,128)(2,1)}, bf16[16,256,256]{2,1,0:T(8,128)(2,1)}, f32[256,1024]{1,0:T(8,128)}, bf16[256,1024]{1,0:T(8,128)(2,1)}) custom-call(bf16[256,1024]{1,0:T(8,128)(2,1)} %copy-done.12, f32[256,1024]{1,0:T(8,128)} %copy-done.1, bf16[16,32,4096]{2,1,0:T(8,128)(2,1)} %all_to_all.5.refs_2_.refs_0_, ...), custom_call_target="tpu_custom_call" | custom-call | tf_op jit(solution)/shard_map/pallas_call | solution.py:357
  130.6 4.8 %all-gather.3.cloned.1.call-done.weights_hbm = bf16[1024,4096]{1,0:T(8,128)(2,1)} async-done(((bf16[32,4096]{1,0:T(8,128)(2,1)}), bf16[1024,4096]{1,0:T(8,128)(2,1)}) %all-gather.3.cloned.1.call-update) | async-done | bytes 8388624 | tf_op jit(solution)/shard_map/all_gather | solution.py:323
  135.4 1.0 copy-done.11
  136.5 7.2 %shard_map.133 = (bf16[128,1024]{1,0:T(8,128)(2,1)S(1)}, bf16[128,1024]{1,0:T(8,128)(2,1)S(1)}, bf16[256,1024]{1,0:T(8,128)(2,1)S(1)}) custom-call(bf16[256,1024]{1,0:T(8,128)(2,1)S(1)} %copy-done.11, bf16[256,1024]{1,0:T(8,128)(2,1)S(1)} %copy-done.5, bf16[1024,4096]{1,0:T(8,128)(2,1)} %all-gather.3.cloned.1.call-done.weights_hbm), custom_call_target="tpu_custom_call" | custom-call | tf_op jit(solution)/shard_map/pallas_call | solution.py:382
  143.7 5.7 %collective-permute-start.2 = (bf16[128,1024]{1,0:T(8,128)(2,1)S(1)}, bf16[128,1024]{1,0:T(8,128)(2,1)S(1)}, u32[]{:S(2)}, u32[]{:S(2)}) collective-permute-start(bf16[128,1024]{1,0:T(8,128)(2,1)S(1)} %get-tuple-element.19.refs_4_), channel_id=1, source_target_pairs={{0,15},{1,0},{2,1},{3,2},{4,3},{5,4},{6,5},{7,6},{8,7},{9,8},{10,9... | collective-permute-start | bytes 786440 | tf_op jit(solution)/shard_map/ppermute | solution.py:403
  149.4 1.9 %collective-permute-start.3 = (bf16[128,1024]{1,0:T(8,128)(2,1)S(1)}, bf16[128,1024]{1,0:T(8,128)(2,1)S(1)}, u32[]{:S(2)}, u32[]{:S(2)}) collective-permute-start(bf16[128,1024]{1,0:T(8,128)(2,1)S(1)} %get-tuple-element.20.refs_6_), channel_id=1, source_target_pairs={{0,1},{1,2},{2,3},{3,4},{4,5},{5,6},{6,7},{7,8},{8,9},{9,10},{10,1... | collective-permute-start | bytes 786440 | tf_op jit(solution)/shard_map/ppermute | solution.py:404
  151.3 2.1 %collective-permute-start.1 = (bf16[256,1024]{1,0:T(8,128)(2,1)S(1)}, bf16[256,1024]{1,0:T(8,128)(2,1)S(1)}, u32[]{:S(2)}, u32[]{:S(2)}) collective-permute-start(bf16[256,1024]{1,0:T(8,128)(2,1)S(1)} %get-tuple-element.18), channel_id=1, source_target_pairs={{0,1},{1,0},{2,3},{3,2},{4,5},{5,4},{6,7},{7,6},{8,9},{9,8},{10,11... | collective-permute-start | bytes 1572872 | tf_op jit(solution)/shard_map/ppermute | solution.py:405
  153.5 1.4 collective-permute-done.2.refs_5_
  154.9 5.0 %collective-permute-done.3.refs_7_ = bf16[128,1024]{1,0:T(8,128)(2,1)S(1)} collective-permute-done((bf16[128,1024]{1,0:T(8,128)(2,1)S(1)}, bf16[128,1024]{1,0:T(8,128)(2,1)S(1)}, u32[]{:S(2)}, u32[]{:S(2)}) %collective-permute-start.3) | collective-permute-done | bytes 262176 | tf_op jit(solution)/shard_map/ppermute | solution.py:404
  159.9 12.4 %shard_map.134 = f32[256,768]{1,0:T(8,128)} custom-call(bf16[16,32,4096]{2,1,0:T(8,128)(2,1)} %all_to_all.5.refs_2_.refs_0_, bf16[16,32,4096]{2,1,0:T(8,128)(2,1)} %bitcast.6.refs_3_.refs_1_, bf16[256,1024]{1,0:T(8,128)(2,1)S(1)} %copy-done.5, f32[256,1024]{1,0:T(8,128)S(1)} %copy-done.3, bf16[128,1024]{1,0:T(8,128)(2,1)S(1)} %get-tuple-element.19.refs_4_, ...), custom_call_target="tpu_custom_call" | custom-call | flops 4294967296 | bytes 20971520 | tf_op jit(solution)/shard_map/pallas_call | solution.py:409
  172.3 1.0 add_convert_fusion
  (42 shorter events, 1.5 us)
Async XLA Ops:
  7.2 128.2 %all-gather.3.cloned.1.call-start = ((), (), s32[]{:S(2)}) async-start(), calls=%async_computation.1 | async-start | bytes 8650752 | tf_op jit(solution)/shard_map/all_gather | solution.py:323
  46.1 66.0 %copy-start.16 = (s32[1,256]{1,0:T(1,128)S(1)}, s32[1,256]{1,0:T(1,128)}, u32[]{:S(2)}) copy-start(s32[1,256]{1,0:T(1,128)} %refs_6_.1) | copy-start | bytes 3076
  46.1 66.8 %copy-start = (bf16[768,1024]{1,0:T(8,128)(2,1)S(1)}, bf16[768,1024]{1,0:T(8,128)(2,1)}, u32[]{:S(2)}) copy-start(bf16[768,1024]{1,0:T(8,128)(2,1)} %refs_12_.1) | copy-start | bytes 4718596
  46.1 66.7 %copy-start.4 = (f32[256,768]{1,0:T(8,128)S(1)}, f32[256,768]{1,0:T(8,128)}, u32[]{:S(2)}) copy-start(f32[256,768]{1,0:T(8,128)} %refs_13_.1) | copy-start | bytes 2359300
  46.1 66.7 %copy-start.10 = (f32[256,768]{1,0:T(8,128)S(1)}, f32[256,768]{1,0:T(8,128)}, u32[]{:S(2)}) copy-start(f32[256,768]{1,0:T(8,128)} %pix_ref.1) | copy-start | bytes 2359300
  46.1 66.7 %copy-start.14 = (f32[1024]{0:T(1024)S(1)}, f32[1024]{0:T(1024)}, u32[]{:S(2)}) copy-start(f32[1024]{0:T(1024)} %param.17) | copy-start | bytes 12292
  101.4 18.1 %collective-permute-start = (bf16[512,4096]{1,0:T(8,128)(2,1)}, bf16[512,4096]{1,0:T(8,128)(2,1)}, u32[]{:S(2)}, u32[]{:S(2)}) collective-permute-start(bf16[512,4096]{1,0:T(8,128)(2,1)} %bitcast.5), channel_id=1, source_target_pairs={{0,16},{16,0},{32,48},{48,32},{64,80},{80,64},{96,112},{112,96},{1... | collective-permute-start | bytes 12582920 | tf_op jit(solution)/shard_map/ppermute | solution.py:330
  113.7 1.0 copy-start.1
  114.7 0.8 copy-start.12
  119.5 15.9 %copy-start.5 = (bf16[256,1024]{1,0:T(8,128)(2,1)S(1)}, bf16[256,1024]{1,0:T(8,128)(2,1)}, u32[]{:S(2)}) copy-start(bf16[256,1024]{1,0:T(8,128)(2,1)} %refs_2_.1) | copy-start | bytes 1572868
  135.4 1.0 copy-start.11
  136.5 23.4 %copy-start.2 = (f32[256,1024]{1,0:T(8,128)S(1)}, f32[256,1024]{1,0:T(8,128)}, u32[]{:S(2)}) copy-start(f32[256,1024]{1,0:T(8,128)} %copy-done.1) | copy-start | bytes 3145732
  136.5 23.4 %copy-start.3 = (f32[256,1024]{1,0:T(8,128)S(1)}, f32[256,1024]{1,0:T(8,128)}, u32[]{:S(2)}) copy-start(f32[256,1024]{1,0:T(8,128)} %get-tuple-element.16.refs_3_) | copy-start | bytes 3145732
  136.5 23.4 %copy-start.6 = (bf16[16,256,256]{2,1,0:T(8,128)(2,1)S(1)}, bf16[16,256,256]{2,1,0:T(8,128)(2,1)}, u32[]{:S(2)}) copy-start(bf16[16,256,256]{2,1,0:T(8,128)(2,1)} %get-tuple-element.22.refs_9_) | copy-start | bytes 6291460
  136.5 23.4 %copy-start.7 = (bf16[16,256,256]{2,1,0:T(8,128)(2,1)S(1)}, bf16[16,256,256]{2,1,0:T(8,128)(2,1)}, u32[]{:S(2)}) copy-start(bf16[16,256,256]{2,1,0:T(8,128)(2,1)} %get-tuple-element.23.refs_10_) | copy-start | bytes 6291460
  136.5 23.4 %copy-start.8 = (bf16[3,256,1024]{2,1,0:T(8,128)(2,1)S(1)}, bf16[3,256,1024]{2,1,0:T(8,128)(2,1)}, u32[]{:S(2)}) copy-start(bf16[3,256,1024]{2,1,0:T(8,128)(2,1)} %get-tuple-element.21.refs_8_) | copy-start | bytes 4718596
  136.5 23.4 %copy-start.9 = (s32[256,1]{1,0:T(8,128)S(1)}, s32[256,1]{1,0:T(8,128)}, u32[]{:S(2)}) copy-start(s32[256,1]{1,0:T(8,128)} %copy.19.refs_5_.refs_17_) | copy-start | bytes 3076
  136.5 23.4 %copy-start.13 = (f32[1024]{0:T(1024)S(1)}, f32[1024]{0:T(1024)}, u32[]{:S(2)}) copy-start(f32[1024]{0:T(1024)} %param.20) | copy-start | bytes 12292
  136.5 23.4 %copy-start.15 = (f32[1,4]{1,0:T(1,128)S(1)}, f32[1,4]{1,0:T(1,128)}, u32[]{:S(2)}) copy-start(f32[1,4]{1,0:T(1,128)} %refs_16_.1) | copy-start | bytes 52
  143.7 11.1 %collective-permute-start.2 = (bf16[128,1024]{1,0:T(8,128)(2,1)S(1)}, bf16[128,1024]{1,0:T(8,128)(2,1)S(1)}, u32[]{:S(2)}, u32[]{:S(2)}) collective-permute-start(bf16[128,1024]{1,0:T(8,128)(2,1)S(1)} %get-tuple-element.19.refs_4_), channel_id=1, source_target_pairs={{0,15},{1,0},{2,1},{3,2},{4,3},{5,4},{6,5},{7,6},{8,7},{9,8},{10,9... | collective-permute-start | bytes 786440 | tf_op jit(solution)/shard_map/ppermute | solution.py:403
  149.4 10.4 %collective-permute-start.3 = (bf16[128,1024]{1,0:T(8,128)(2,1)S(1)}, bf16[128,1024]{1,0:T(8,128)(2,1)S(1)}, u32[]{:S(2)}, u32[]{:S(2)}) collective-permute-start(bf16[128,1024]{1,0:T(8,128)(2,1)S(1)} %get-tuple-element.20.refs_6_), channel_id=1, source_target_pairs={{0,1},{1,2},{2,3},{3,4},{4,5},{5,6},{6,7},{7,8},{8,9},{9,10},{10,1... | collective-permute-start | bytes 786440 | tf_op jit(solution)/shard_map/ppermute | solution.py:404
  151.3 21.0 %collective-permute-start.1 = (bf16[256,1024]{1,0:T(8,128)(2,1)S(1)}, bf16[256,1024]{1,0:T(8,128)(2,1)S(1)}, u32[]{:S(2)}, u32[]{:S(2)}) collective-permute-start(bf16[256,1024]{1,0:T(8,128)(2,1)S(1)} %get-tuple-element.18), channel_id=1, source_target_pairs={{0,1},{1,0},{2,3},{3,2},{4,5},{5,4},{6,7},{7,6},{8,9},{9,8},{10,11... | collective-permute-start | bytes 1572872 | tf_op jit(solution)/shard_map/ppermute | solution.py:405
Sparse Core Ops, SparseCore 0:
  44.4 91.0 all-gather.2
